TPU v7x, 256 devices: a whole 4x4x8 slice. The times are simulated.
256 devices in a mesh: section: 8 (over x_lo, y), seq: 16 (over z, core), dp: 2 (over x_hi).
Axes of the slice: x: 4 (x_hi: 2, x_lo: 2; x = x_hi * 2 + x_lo), y: 4, z: 8, core: 2. Of those that a mesh axis runs over, the one named last changes fastest.
Arguments:
- mel: bfloat16 [4, 8192, 128], P('dp', 'seq'), may hold values from -6 to 6
- lengths: int32 [4], P('dp'), may hold values from 1024 to 2048, as said below
- stem_weight: bfloat16 [512, 1536], P(('seq', 'dp')), may hold values from -0.25 to 0.25
- w_qkv: bfloat16 [8, 1536, 2304], P('section', ('seq', 'dp'))
- w_out: bfloat16 [8, 768, 1536], P('section', ('seq', 'dp')), may hold values from -0.21875 to 0.21875
- norm_gains: float32 [8, 2, 1536], P('section'), may hold values from 0.25 to 1.75
- conv_kernel: float32 [8, 5, 1536], P('section'), may hold values from -2.5 to 2.5
Outputs:
- arrivals: bfloat16 [8, 4, 2048, 1536], P('section', 'dp', 'seq')
Inputs may be any that keep to these rules, and one draw needn't show every extreme that they name: `lengths`: every utterance keeps at least half of its 2048 frames; one utterance of each draw keeps all of them.
All inputs are finite; a program needn't handle non-finite values.
Results may differ from a plain program's by a relative error of at most 0.029.
Values may be sent and summed in bfloat16 or wider, within the bound.
A program may use at most 64 MiB of HBM per device.

v0:
```python
import jax
import jax.numpy as jnp
from jax import lax
from jax.sharding import PartitionSpec as P

HEADS = 8
STRIDE = 4


eps = 1e-05
masked_score = -1e30


def extended(block, sides, width):
    for axis, dim in sides:
        count = lax.axis_size(axis)
        forward = [(i, i + 1) for i in range(count - 1)]
        backward = [(target, source) for source, target in forward]
        low = lax.ppermute(
            lax.slice_in_dim(block, block.shape[dim] - width, None, axis=dim), axis, forward
        )
        high = lax.ppermute(lax.slice_in_dim(block, 0, width, axis=dim), axis, backward)
        block = jnp.concatenate([low, block, high], axis=dim)
    return block


def from_behind(value, axis, steps):
    count = lax.axis_size(axis)
    pairs = [(source, (source + steps) % count) for source in range(count)]
    return lax.ppermute(value, axis, pairs)


def layer_norm(value, gain):
    average = jnp.mean(value, axis=-1, keepdims=True)
    centered = value - average
    variance = jnp.mean(centered * centered, axis=-1, keepdims=True)
    return centered * lax.rsqrt(variance + eps) * gain


def band_attention(queries, keys_values, first_query, length, heads):
    frames = queries.shape[0]
    width = queries.shape[1]
    head_size = width // heads
    span = keys_values.shape[0]
    query_rows = queries.reshape(frames, heads, head_size)
    key_rows = keys_values[:, :width].reshape(span, heads, head_size)
    value_rows = keys_values[:, width:].reshape(span, heads, head_size)
    scores = jnp.einsum(
        "qhd,khd->hqk", query_rows, key_rows, preferred_element_type=jnp.float32
    ) * (1.0 / head_size**0.5)
    query_pos = first_query + jnp.arange(frames, dtype=jnp.int32)
    key_pos = first_query - frames + jnp.arange(span, dtype=jnp.int32)
    allowed = (
        (key_pos[None, :] >= 0)
        & (key_pos[None, :] < length)
        & (jnp.abs(query_pos[:, None] - key_pos[None, :]) <= frames)
    )
    scores = jnp.where(allowed[None], scores, masked_score)
    highest = jnp.max(scores, axis=-1, keepdims=True)
    expon = jnp.exp(scores - highest)
    probs = (expon / jnp.sum(expon, axis=-1, keepdims=True)).astype(jnp.bfloat16)
    context = jnp.einsum("hqk,khd->qhd", probs, value_rows, preferred_element_type=jnp.float32)
    return context.astype(jnp.bfloat16).reshape(frames, width)


def apply_layer(held_input, valid, length, first_query, full_qkv, full_out, gains, kernel):
    frames = held_input.shape[0]
    width = full_out.shape[0]
    stream = held_input.astype(jnp.float32)
    normed = layer_norm(stream, gains[0]).astype(jnp.bfloat16)
    qkv = jnp.dot(normed, full_qkv, preferred_element_type=jnp.float32).astype(jnp.bfloat16)
    nearby = extended(qkv[:, width:], (("seq", 0),), frames)
    context = band_attention(qkv[:, :width], nearby, first_query, length, HEADS)
    stream = stream + jnp.dot(context, full_out, preferred_element_type=jnp.float32)
    conv_in = (layer_norm(stream, gains[1]) * valid[:, None]).astype(jnp.bfloat16)
    taps = kernel.shape[0]
    padded = extended(conv_in, (("seq", 0),), taps // 2)
    conv = jnp.zeros(stream.shape, jnp.float32)
    for offset in range(taps):
        conv = conv + padded[offset : offset + frames].astype(jnp.float32) * kernel[offset]
    return ((stream + jax.nn.silu(conv)) * valid[:, None]).astype(jnp.bfloat16)


def place_row(buffer, value, index):
    inside = (index >= 0) & (index < buffer.shape[0])
    clipped = jnp.clip(index, 0, buffer.shape[0] - 1)
    previous = lax.dynamic_index_in_dim(buffer, clipped, 0, keepdims=True)
    return lax.dynamic_update_index_in_dim(
        buffer, jnp.where(inside, value[None], previous), clipped, 0
    )


def shards(mel, lengths, stem_weight, w_qkv, w_out, norm_gains, conv_kernel):
    sections = lax.axis_size("section")
    section_index = lax.axis_index("section")
    seq_index = lax.axis_index("seq")
    micro = mel.shape[0]
    frames = mel.shape[1] // STRIDE
    full_stem, full_qkv, full_out = (
        lax.all_gather(stem_weight, ("seq", "dp"), axis=0, tiled=True),
        lax.all_gather(w_qkv, ("seq", "dp"), axis=1, tiled=True),
        lax.all_gather(w_out, ("seq", "dp"), axis=1, tiled=True),
    )
    full_qkv = full_qkv[0]
    full_out = full_out[0]
    gains = norm_gains[0]
    kernel = conv_kernel[0]
    model_width = full_out.shape[1]
    first_query = seq_index * frames
    positions = first_query + jnp.arange(frames, dtype=jnp.int32)
    valid_all = (positions[None, :] < lengths[:, None]).astype(jnp.float32)
    ticks = micro + sections - 1

    def tick(tick_index, carry):
        held_input, arrived, finished = carry
        micro_now = tick_index - section_index
        micro_slot = jnp.clip(micro_now, 0, micro - 1)
        valid = lax.dynamic_index_in_dim(valid_all, micro_slot, 0, keepdims=False)
        length = lax.dynamic_index_in_dim(lengths, micro_slot, 0, keepdims=False)

        def from_stem(operands):
            slot, mask, unused = operands
            grouped = lax.dynamic_index_in_dim(mel, slot, 0, keepdims=False).reshape(
                frames, STRIDE * mel.shape[2]
            )
            stem_out = (
                jax.nn.silu(jnp.dot(grouped, full_stem, preferred_element_type=jnp.float32))
                * mask[:, None]
            )
            return stem_out.astype(jnp.bfloat16)

        def from_before(operands):
            return operands[2]

        layer_input = lax.cond(
            section_index == 0, from_stem, from_before, (micro_slot, valid, held_input)
        )
        output = apply_layer(
            layer_input, valid, length, first_query, full_qkv, full_out, gains, kernel
        )
        received = from_behind(output, "section", 1)
        arriving = jnp.where(
            section_index == 0, tick_index - sections + 1, tick_index - section_index + 1
        )
        arrived = place_row(arrived, received, arriving)
        return (received, arrived, finished)

    start_input = jnp.zeros((frames, model_width), jnp.bfloat16)
    start_rows = jnp.zeros((micro, frames, model_width), jnp.bfloat16)
    held_input, arrived, finished = lax.fori_loop(
        0, ticks, tick, (start_input, start_rows, start_rows)
    )
    return arrived[None]


def solution(mesh):
    return jax.shard_map(
        shards,
        mesh=mesh,
        in_specs=(
            P("dp", "seq", None),
            P("dp"),
            P(("seq", "dp"), None),
            P("section", ("seq", "dp"), None),
            P("section", ("seq", "dp"), None),
            P("section", None, None),
            P("section", None, None),
        ),
        out_specs=P("section", "dp", "seq", None),
        check_vma=False,
    )
```

profile of v0, /device:TPU:1, one launch (start us, length us, event | category | flops | bytes accessed | tf_op | source)
XLA Modules:
  0.0 677.8 jit_solution(6024125961725418431)
XLA Ops:
  10.2 82.9 %all-gather.4.cloned.1.call-done = bf16[512,1536]{1,0:T(8,128)(2,1)} async-done(((bf16[16,1536]{1,0:T(8,128)(2,1)}), bf16[512,1536]{1,0:T(8,128)(2,1)}) %all-gather.4.cloned.1.call-update) | async-done | bytes 1572880 | tf_op jit(solution)/shard_map/all_gather | solution.py:100
  93.2 80.0 %all-gather.8.cloned.1.call-done = bf16[1,768,1536]{2,1,0:T(8,128)(2,1)} async-done(((bf16[1,24,1536]{2,1,0:T(8,128)(2,1)}), bf16[1,768,1536]{2,1,0:T(8,128)(2,1)}) %all-gather.8.cloned.1.call-update) | async-done | bytes 2359312 | tf_op jit(solution)/shard_map/all_gather | solution.py:102
  173.2 96.5 %all-gather.6.cloned.1.call-done = bf16[1,1536,2304]{2,1,0:T(8,128)(2,1)} async-done(((bf16[1,48,2304]{2,1,0:T(8,128)(2,1)}), bf16[1,1536,2304]{2,1,0:T(8,128)(2,1)}) %all-gather.6.cloned.1.call-update) | async-done | bytes 7077904 | tf_op jit(solution)/shard_map/all_gather | solution.py:101
  270.7 400.6 %while.23 = (s32[]{:T(128)}, bf16[128,1536]{1,0:T(8,128)(2,1)S(1)}, bf16[2,128,1536]{2,1,0:T(8,128)(2,1)}, pred[]{:T(512)}, s32[]{:T(128)}, /*index=5*/f32[2,128...) while((s32[]{:T(128)}, bf16[128,1536]{1,0:T(8,128)(2,1)S(1)}, ...), condition=%wide.region_10.11_spmd, body=%wide.region_0.10_spmd.sunk | while | flops 1578371712 | bytes 55258044 | solution.py:150
  270.7 2.1 conditional.2
  273.1 4.2 convolution_convert_fusion.4
  277.3 2.2 collective-permute-start
  279.5 3.4 collective-permute-start.1
  284.5 1.9 collective-permute-done
  290.3 2.1 convolution_convert_fusion.5
  295.5 4.4 collective-permute-start.3
  301.5 11.5 %collective-permute-done.4 = bf16[128,1536]{1,0:T(8,128)(2,1)S(1)} collective-permute-done((bf16[128,1536]{1,0:T(8,128)(2,1)S(1)}, bf16[128,1536]{1,0:T(8,128)(2,1)S(1)}, u32[]{:S(2)}, u32[]{:S(2)}) %collective-permute-start.4) | collective-permute-done | bytes 393248 | tf_op jit(solution)/shard_map/while/body/eval_jaxpr/ppermute | solution.py:30
  313.9 2.0 conditional.2
  316.3 4.2 convolution_convert_fusion.4
  322.4 5.0 collective-permute-start.1
  329.0 1.9 collective-permute-done
  334.8 2.1 convolution_convert_fusion.5
  340.1 4.4 collective-permute-start.3
  346.0 11.5 %collective-permute-done.4 = bf16[128,1536]{1,0:T(8,128)(2,1)S(1)} collective-permute-done((bf16[128,1536]{1,0:T(8,128)(2,1)S(1)}, bf16[128,1536]{1,0:T(8,128)(2,1)S(1)}, u32[]{:S(2)}, u32[]{:S(2)}) %collective-permute-start.4) | collective-permute-done | bytes 393248 | tf_op jit(solution)/shard_map/while/body/eval_jaxpr/ppermute | solution.py:30
  358.5 2.1 conditional.2
  360.8 4.2 convolution_convert_fusion.4
  367.0 4.5 collective-permute-start.1
  373.1 1.9 collective-permute-done
  378.9 2.1 convolution_convert_fusion.5
  384.1 4.4 collective-permute-start.3
  390.1 11.5 %collective-permute-done.4 = bf16[128,1536]{1,0:T(8,128)(2,1)S(1)} collective-permute-done((bf16[128,1536]{1,0:T(8,128)(2,1)S(1)}, bf16[128,1536]{1,0:T(8,128)(2,1)S(1)}, u32[]{:S(2)}, u32[]{:S(2)}) %collective-permute-start.4) | collective-permute-done | bytes 393248 | tf_op jit(solution)/shard_map/while/body/eval_jaxpr/ppermute | solution.py:30
  402.6 2.0 conditional.2
  404.9 4.2 convolution_convert_fusion.4
  411.1 5.6 collective-permute-start.1
  424.0 2.1 convolution_convert_fusion.5
  429.3 4.4 collective-permute-start.3
  435.2 11.5 %collective-permute-done.4 = bf16[128,1536]{1,0:T(8,128)(2,1)S(1)} collective-permute-done((bf16[128,1536]{1,0:T(8,128)(2,1)S(1)}, bf16[128,1536]{1,0:T(8,128)(2,1)S(1)}, u32[]{:S(2)}, u32[]{:S(2)}) %collective-permute-start.4) | collective-permute-done | bytes 393248 | tf_op jit(solution)/shard_map/while/body/eval_jaxpr/ppermute | solution.py:30
  447.7 2.0 conditional.2
  450.1 4.2 convolution_convert_fusion.4
  456.2 4.8 collective-permute-start.1
  468.4 2.1 convolution_convert_fusion.5
  473.7 4.4 collective-permute-start.3
  479.6 11.5 %collective-permute-done.4 = bf16[128,1536]{1,0:T(8,128)(2,1)S(1)} collective-permute-done((bf16[128,1536]{1,0:T(8,128)(2,1)S(1)}, bf16[128,1536]{1,0:T(8,128)(2,1)S(1)}, u32[]{:S(2)}, u32[]{:S(2)}) %collective-permute-start.4) | collective-permute-done | bytes 393248 | tf_op jit(solution)/shard_map/while/body/eval_jaxpr/ppermute | solution.py:30
  492.1 2.0 conditional.2
  494.4 4.2 convolution_convert_fusion.4
  500.6 4.4 collective-permute-start.1
  512.4 2.1 convolution_convert_fusion.5
  517.6 4.4 collective-permute-start.3
  523.6 11.5 %collective-permute-done.4 = bf16[128,1536]{1,0:T(8,128)(2,1)S(1)} collective-permute-done((bf16[128,1536]{1,0:T(8,128)(2,1)S(1)}, bf16[128,1536]{1,0:T(8,128)(2,1)S(1)}, u32[]{:S(2)}, u32[]{:S(2)}) %collective-permute-start.4) | collective-permute-done | bytes 393248 | tf_op jit(solution)/shard_map/while/body/eval_jaxpr/ppermute | solution.py:30
  536.1 2.0 conditional.2
  538.4 4.2 convolution_convert_fusion.4
  544.6 5.3 collective-permute-start.1
  551.5 1.9 collective-permute-done
  557.3 2.1 convolution_convert_fusion.5
  562.5 4.4 collective-permute-start.3
  568.5 11.5 %collective-permute-done.4 = bf16[128,1536]{1,0:T(8,128)(2,1)S(1)} collective-permute-done((bf16[128,1536]{1,0:T(8,128)(2,1)S(1)}, bf16[128,1536]{1,0:T(8,128)(2,1)S(1)}, u32[]{:S(2)}, u32[]{:S(2)}) %collective-permute-start.4) | collective-permute-done | bytes 393248 | tf_op jit(solution)/shard_map/while/body/eval_jaxpr/ppermute | solution.py:30
  580.9 2.0 conditional.2
  583.3 4.2 convolution_convert_fusion.4
  589.4 5.7 collective-permute-start.1
  602.5 2.1 convolution_convert_fusion.5
  607.7 4.4 collective-permute-start.3
  613.7 11.5 %collective-permute-done.4 = bf16[128,1536]{1,0:T(8,128)(2,1)S(1)} collective-permute-done((bf16[128,1536]{1,0:T(8,128)(2,1)S(1)}, bf16[128,1536]{1,0:T(8,128)(2,1)S(1)}, u32[]{:S(2)}, u32[]{:S(2)}) %collective-permute-start.4) | collective-permute-done | bytes 393248 | tf_op jit(solution)/shard_map/while/body/eval_jaxpr/ppermute | solution.py:30
  626.1 2.0 conditional.2
  628.5 4.2 convolution_convert_fusion.4
  634.6 5.6 collective-permute-start.1
  641.9 1.9 collective-permute-done
  647.6 2.1 convolution_convert_fusion.5
  652.9 4.4 collective-permute-start.3
  658.8 11.5 %collective-permute-done.4 = bf16[128,1536]{1,0:T(8,128)(2,1)S(1)} collective-permute-done((bf16[128,1536]{1,0:T(8,128)(2,1)S(1)}, bf16[128,1536]{1,0:T(8,128)(2,1)S(1)}, u32[]{:S(2)}, u32[]{:S(2)}) %collective-permute-start.4) | collective-permute-done | bytes 393248 | tf_op jit(solution)/shard_map/while/body/eval_jaxpr/ppermute | solution.py:30
  (398 shorter events, 147.5 us)
Async XLA Ops:
  6.5 264.1 %copy-start.5 = (s32[2]{0:T(128)S(1)}, s32[2]{0:T(128)}, u32[]{:S(2)}) copy-start(s32[2]{0:T(128)} %param.12) | copy-start | bytes 28
  6.5 264.1 %copy-start.4 = (f32[1,2,1536]{2,1,0:T(2,128)S(1)}, f32[1,2,1536]{2,1,0:T(2,128)}, u32[]{:S(2)}) copy-start(f32[1,2,1536]{2,1,0:T(2,128)} %param.16) | copy-start | bytes 36868
  6.5 264.2 %copy-start.3 = (bf16[2,512,128]{2,1,0:T(8,128)(2,1)S(1)}, bf16[2,512,128]{2,1,0:T(8,128)(2,1)}, u32[]{:S(2)}) copy-start(bf16[2,512,128]{2,1,0:T(8,128)(2,1)} %param.11) | copy-start | bytes 786436
  6.5 86.6 %all-gather.4.cloned.1.call-start = ((), (), s32[]{:S(2)}) async-start(), calls=%async_computation | async-start | bytes 1622016 | tf_op jit(solution)/shard_map/all_gather | solution.py:100
  7.3 165.9 %all-gather.8.cloned.1.call-start = ((), (), s32[]{:S(2)}) async-start(), calls=%async_computation.2 | async-start | bytes 2433024 | tf_op jit(solution)/shard_map/all_gather | solution.py:102
  8.0 261.7 %all-gather.6.cloned.1.call-start = ((), (), s32[]{:S(2)}) async-start(), calls=%async_computation.1 | async-start | bytes 7299072 | tf_op jit(solution)/shard_map/all_gather | solution.py:101
  277.3 9.1 %collective-permute-start = (bf16[128,1536]{1,0:T(8,128)(2,1)S(1)}, bf16[128,1536]{1,0:T(8,128)(2,1)S(1)}, u32[]{:S(2)}, u32[]{:S(2)}) collective-permute-start(bf16[128,1536]{1,0:T(8,128)(2,1)S(1)} %slice.284), channel_id=1, source_target_pairs={{2,0},{4,2},{6,4},{8,6},{10,8},{12,10},{14,12},{16,14},{18,16},{20... | collective-permute-start | bytes 1179656 | tf_op jit(solution)/shard_map/while/body/eval_jaxpr/ppermute | solution.py:22
  279.5 8.1 %collective-permute-start.1 = (bf16[128,1536]{1,0:T(8,128)(2,1)S(1)}, bf16[128,1536]{1,0:T(8,128)(2,1)S(1)}, u32[]{:S(2)}, u32[]{:S(2)}) collective-permute-start(bf16[128,1536]{1,0:T(8,128)(2,1)S(1)} %slice.284), channel_id=1, source_target_pairs={{0,2},{2,4},{4,6},{6,8},{8,10},{10,12},{12,14},{14,16},{16,18},{18... | collective-permute-start | bytes 1179656 | tf_op jit(solution)/shard_map/while/body/eval_jaxpr/ppermute | solution.py:19
  293.2 19.7 %copy-start.1 = (bf16[2,128,1536]{2,1,0:T(8,128)(2,1)S(1)}, bf16[2,128,1536]{2,1,0:T(8,128)(2,1)}, u32[]{:S(2)}) copy-start(bf16[2,128,1536]{2,1,0:T(8,128)(2,1)} %get-tuple-element.687) | copy-start | bytes 2359300 | tf_op jit(solution)/shard_map/while
  293.6 6.4 collective-permute-start.2
  295.5 5.1 collective-permute-start.3
  301.4 11.6 %collective-permute-start.4 = (bf16[128,1536]{1,0:T(8,128)(2,1)S(1)}, bf16[128,1536]{1,0:T(8,128)(2,1)S(1)}, u32[]{:S(2)}, u32[]{:S(2)}) collective-permute-start(bf16[128,1536]{1,0:T(8,128)(2,1)S(1)} %multiply_convert_fusion.10), channel_id=1, source_target_pairs={{0,32},{32,64},{64,96},{96,128},{128,160},{160,192},{192,224},{224... | collective-permute-start | bytes 1179656 | tf_op jit(solution)/shard_map/while/body/eval_jaxpr/ppermute | solution.py:30
  320.5 10.5 %collective-permute-start = (bf16[128,1536]{1,0:T(8,128)(2,1)S(1)}, bf16[128,1536]{1,0:T(8,128)(2,1)S(1)}, u32[]{:S(2)}, u32[]{:S(2)}) collective-permute-start(bf16[128,1536]{1,0:T(8,128)(2,1)S(1)} %slice.284), channel_id=1, source_target_pairs={{2,0},{4,2},{6,4},{8,6},{10,8},{12,10},{14,12},{16,14},{18,16},{20... | collective-permute-start | bytes 1179656 | tf_op jit(solution)/shard_map/while/body/eval_jaxpr/ppermute | solution.py:22
  322.4 9.7 %collective-permute-start.1 = (bf16[128,1536]{1,0:T(8,128)(2,1)S(1)}, bf16[128,1536]{1,0:T(8,128)(2,1)S(1)}, u32[]{:S(2)}, u32[]{:S(2)}) collective-permute-start(bf16[128,1536]{1,0:T(8,128)(2,1)S(1)} %slice.284), channel_id=1, source_target_pairs={{0,2},{2,4},{4,6},{6,8},{8,10},{10,12},{12,14},{14,16},{16,18},{18... | collective-permute-start | bytes 1179656 | tf_op jit(solution)/shard_map/while/body/eval_jaxpr/ppermute | solution.py:19
  334.8 2.1 copy-start
  337.8 19.7 %copy-start.1 = (bf16[2,128,1536]{2,1,0:T(8,128)(2,1)S(1)}, bf16[2,128,1536]{2,1,0:T(8,128)(2,1)}, u32[]{:S(2)}) copy-start(bf16[2,128,1536]{2,1,0:T(8,128)(2,1)} %get-tuple-element.687) | copy-start | bytes 2359300 | tf_op jit(solution)/shard_map/while
  338.1 6.4 collective-permute-start.2
  340.1 5.1 collective-permute-start.3
  345.9 11.6 %collective-permute-start.4 = (bf16[128,1536]{1,0:T(8,128)(2,1)S(1)}, bf16[128,1536]{1,0:T(8,128)(2,1)S(1)}, u32[]{:S(2)}, u32[]{:S(2)}) collective-permute-start(bf16[128,1536]{1,0:T(8,128)(2,1)S(1)} %multiply_convert_fusion.10), channel_id=1, source_target_pairs={{0,32},{32,64},{64,96},{96,128},{128,160},{160,192},{192,224},{224... | collective-permute-start | bytes 1179656 | tf_op jit(solution)/shard_map/while/body/eval_jaxpr/ppermute | solution.py:30
  365.1 10.0 %collective-permute-start = (bf16[128,1536]{1,0:T(8,128)(2,1)S(1)}, bf16[128,1536]{1,0:T(8,128)(2,1)S(1)}, u32[]{:S(2)}, u32[]{:S(2)}) collective-permute-start(bf16[128,1536]{1,0:T(8,128)(2,1)S(1)} %slice.284), channel_id=1, source_target_pairs={{2,0},{4,2},{6,4},{8,6},{10,8},{12,10},{14,12},{16,14},{18,16},{20... | collective-permute-start | bytes 1179656 | tf_op jit(solution)/shard_map/while/body/eval_jaxpr/ppermute | solution.py:22
  367.0 9.2 %collective-permute-start.1 = (bf16[128,1536]{1,0:T(8,128)(2,1)S(1)}, bf16[128,1536]{1,0:T(8,128)(2,1)S(1)}, u32[]{:S(2)}, u32[]{:S(2)}) collective-permute-start(bf16[128,1536]{1,0:T(8,128)(2,1)S(1)} %slice.284), channel_id=1, source_target_pairs={{0,2},{2,4},{4,6},{6,8},{8,10},{10,12},{12,14},{14,16},{16,18},{18... | collective-permute-start | bytes 1179656 | tf_op jit(solution)/shard_map/while/body/eval_jaxpr/ppermute | solution.py:19
  378.9 2.1 copy-start
  381.9 19.7 %copy-start.1 = (bf16[2,128,1536]{2,1,0:T(8,128)(2,1)S(1)}, bf16[2,128,1536]{2,1,0:T(8,128)(2,1)}, u32[]{:S(2)}) copy-start(bf16[2,128,1536]{2,1,0:T(8,128)(2,1)} %get-tuple-element.687) | copy-start | bytes 2359300 | tf_op jit(solution)/shard_map/while
  382.2 6.4 collective-permute-start.2
  384.1 5.1 collective-permute-start.3
  390.0 11.6 %collective-permute-start.4 = (bf16[128,1536]{1,0:T(8,128)(2,1)S(1)}, bf16[128,1536]{1,0:T(8,128)(2,1)S(1)}, u32[]{:S(2)}, u32[]{:S(2)}) collective-permute-start(bf16[128,1536]{1,0:T(8,128)(2,1)S(1)} %multiply_convert_fusion.10), channel_id=1, source_target_pairs={{0,32},{32,64},{64,96},{96,128},{128,160},{160,192},{192,224},{224... | collective-permute-start | bytes 1179656 | tf_op jit(solution)/shard_map/while/body/eval_jaxpr/ppermute | solution.py:30
  409.1 11.1 %collective-permute-start = (bf16[128,1536]{1,0:T(8,128)(2,1)S(1)}, bf16[128,1536]{1,0:T(8,128)(2,1)S(1)}, u32[]{:S(2)}, u32[]{:S(2)}) collective-permute-start(bf16[128,1536]{1,0:T(8,128)(2,1)S(1)} %slice.284), channel_id=1, source_target_pairs={{2,0},{4,2},{6,4},{8,6},{10,8},{12,10},{14,12},{16,14},{18,16},{20... | collective-permute-start | bytes 1179656 | tf_op jit(solution)/shard_map/while/body/eval_jaxpr/ppermute | solution.py:22
  411.1 10.3 %collective-permute-start.1 = (bf16[128,1536]{1,0:T(8,128)(2,1)S(1)}, bf16[128,1536]{1,0:T(8,128)(2,1)S(1)}, u32[]{:S(2)}, u32[]{:S(2)}) collective-permute-start(bf16[128,1536]{1,0:T(8,128)(2,1)S(1)} %slice.284), channel_id=1, source_target_pairs={{0,2},{2,4},{4,6},{6,8},{8,10},{10,12},{12,14},{14,16},{16,18},{18... | collective-permute-start | bytes 1179656 | tf_op jit(solution)/shard_map/while/body/eval_jaxpr/ppermute | solution.py:19
  424.0 2.1 copy-start
  427.0 19.7 %copy-start.1 = (bf16[2,128,1536]{2,1,0:T(8,128)(2,1)S(1)}, bf16[2,128,1536]{2,1,0:T(8,128)(2,1)}, u32[]{:S(2)}) copy-start(bf16[2,128,1536]{2,1,0:T(8,128)(2,1)} %get-tuple-element.687) | copy-start | bytes 2359300 | tf_op jit(solution)/shard_map/while
  427.4 6.4 collective-permute-start.2
  429.3 5.1 collective-permute-start.3
  435.1 11.6 %collective-permute-start.4 = (bf16[128,1536]{1,0:T(8,128)(2,1)S(1)}, bf16[128,1536]{1,0:T(8,128)(2,1)S(1)}, u32[]{:S(2)}, u32[]{:S(2)}) collective-permute-start(bf16[128,1536]{1,0:T(8,128)(2,1)S(1)} %multiply_convert_fusion.10), channel_id=1, source_target_pairs={{0,32},{32,64},{64,96},{96,128},{128,160},{160,192},{192,224},{224... | collective-permute-start | bytes 1179656 | tf_op jit(solution)/shard_map/while/body/eval_jaxpr/ppermute | solution.py:30
  454.3 10.3 %collective-permute-start = (bf16[128,1536]{1,0:T(8,128)(2,1)S(1)}, bf16[128,1536]{1,0:T(8,128)(2,1)S(1)}, u32[]{:S(2)}, u32[]{:S(2)}) collective-permute-start(bf16[128,1536]{1,0:T(8,128)(2,1)S(1)} %slice.284), channel_id=1, source_target_pairs={{2,0},{4,2},{6,4},{8,6},{10,8},{12,10},{14,12},{16,14},{18,16},{20... | collective-permute-start | bytes 1179656 | tf_op jit(solution)/shard_map/while/body/eval_jaxpr/ppermute | solution.py:22
  456.2 9.5 %collective-permute-start.1 = (bf16[128,1536]{1,0:T(8,128)(2,1)S(1)}, bf16[128,1536]{1,0:T(8,128)(2,1)S(1)}, u32[]{:S(2)}, u32[]{:S(2)}) collective-permute-start(bf16[128,1536]{1,0:T(8,128)(2,1)S(1)} %slice.284), channel_id=1, source_target_pairs={{0,2},{2,4},{4,6},{6,8},{8,10},{10,12},{12,14},{14,16},{16,18},{18... | collective-permute-start | bytes 1179656 | tf_op jit(solution)/shard_map/while/body/eval_jaxpr/ppermute | solution.py:19
  468.4 2.1 copy-start
  471.4 19.7 %copy-start.1 = (bf16[2,128,1536]{2,1,0:T(8,128)(2,1)S(1)}, bf16[2,128,1536]{2,1,0:T(8,128)(2,1)}, u32[]{:S(2)}) copy-start(bf16[2,128,1536]{2,1,0:T(8,128)(2,1)} %get-tuple-element.687) | copy-start | bytes 2359300 | tf_op jit(solution)/shard_map/while
  471.7 6.4 collective-permute-start.2
  473.7 5.1 collective-permute-start.3
  479.5 11.6 %collective-permute-start.4 = (bf16[128,1536]{1,0:T(8,128)(2,1)S(1)}, bf16[128,1536]{1,0:T(8,128)(2,1)S(1)}, u32[]{:S(2)}, u32[]{:S(2)}) collective-permute-start(bf16[128,1536]{1,0:T(8,128)(2,1)S(1)} %multiply_convert_fusion.10), channel_id=1, source_target_pairs={{0,32},{32,64},{64,96},{96,128},{128,160},{160,192},{192,224},{224... | collective-permute-start | bytes 1179656 | tf_op jit(solution)/shard_map/while/body/eval_jaxpr/ppermute | solution.py:30
  498.7 9.9 %collective-permute-start = (bf16[128,1536]{1,0:T(8,128)(2,1)S(1)}, bf16[128,1536]{1,0:T(8,128)(2,1)S(1)}, u32[]{:S(2)}, u32[]{:S(2)}) collective-permute-start(bf16[128,1536]{1,0:T(8,128)(2,1)S(1)} %slice.284), channel_id=1, source_target_pairs={{2,0},{4,2},{6,4},{8,6},{10,8},{12,10},{14,12},{16,14},{18,16},{20... | collective-permute-start | bytes 1179656 | tf_op jit(solution)/shard_map/while/body/eval_jaxpr/ppermute | solution.py:22
  500.6 9.2 %collective-permute-start.1 = (bf16[128,1536]{1,0:T(8,128)(2,1)S(1)}, bf16[128,1536]{1,0:T(8,128)(2,1)S(1)}, u32[]{:S(2)}, u32[]{:S(2)}) collective-permute-start(bf16[128,1536]{1,0:T(8,128)(2,1)S(1)} %slice.284), channel_id=1, source_target_pairs={{0,2},{2,4},{4,6},{6,8},{8,10},{10,12},{12,14},{14,16},{16,18},{18... | collective-permute-start | bytes 1179656 | tf_op jit(solution)/shard_map/while/body/eval_jaxpr/ppermute | solution.py:19
  515.4 19.7 %copy-start.1 = (bf16[2,128,1536]{2,1,0:T(8,128)(2,1)S(1)}, bf16[2,128,1536]{2,1,0:T(8,128)(2,1)}, u32[]{:S(2)}) copy-start(bf16[2,128,1536]{2,1,0:T(8,128)(2,1)} %get-tuple-element.687) | copy-start | bytes 2359300 | tf_op jit(solution)/shard_map/while
  515.7 6.4 collective-permute-start.2
  517.6 5.1 collective-permute-start.3
  523.5 11.6 %collective-permute-start.4 = (bf16[128,1536]{1,0:T(8,128)(2,1)S(1)}, bf16[128,1536]{1,0:T(8,128)(2,1)S(1)}, u32[]{:S(2)}, u32[]{:S(2)}) collective-permute-start(bf16[128,1536]{1,0:T(8,128)(2,1)S(1)} %multiply_convert_fusion.10), channel_id=1, source_target_pairs={{0,32},{32,64},{64,96},{96,128},{128,160},{160,192},{192,224},{224... | collective-permute-start | bytes 1179656 | tf_op jit(solution)/shard_map/while/body/eval_jaxpr/ppermute | solution.py:30
  542.7 10.8 %collective-permute-start = (bf16[128,1536]{1,0:T(8,128)(2,1)S(1)}, bf16[128,1536]{1,0:T(8,128)(2,1)S(1)}, u32[]{:S(2)}, u32[]{:S(2)}) collective-permute-start(bf16[128,1536]{1,0:T(8,128)(2,1)S(1)} %slice.284), channel_id=1, source_target_pairs={{2,0},{4,2},{6,4},{8,6},{10,8},{12,10},{14,12},{16,14},{18,16},{20... | collective-permute-start | bytes 1179656 | tf_op jit(solution)/shard_map/while/body/eval_jaxpr/ppermute | solution.py:22
  544.6 10.0 %collective-permute-start.1 = (bf16[128,1536]{1,0:T(8,128)(2,1)S(1)}, bf16[128,1536]{1,0:T(8,128)(2,1)S(1)}, u32[]{:S(2)}, u32[]{:S(2)}) collective-permute-start(bf16[128,1536]{1,0:T(8,128)(2,1)S(1)} %slice.284), channel_id=1, source_target_pairs={{0,2},{2,4},{4,6},{6,8},{8,10},{10,12},{12,14},{14,16},{16,18},{18... | collective-permute-start | bytes 1179656 | tf_op jit(solution)/shard_map/while/body/eval_jaxpr/ppermute | solution.py:19
  560.2 19.7 %copy-start.1 = (bf16[2,128,1536]{2,1,0:T(8,128)(2,1)S(1)}, bf16[2,128,1536]{2,1,0:T(8,128)(2,1)}, u32[]{:S(2)}) copy-start(bf16[2,128,1536]{2,1,0:T(8,128)(2,1)} %get-tuple-element.687) | copy-start | bytes 2359300 | tf_op jit(solution)/shard_map/while
  560.6 6.4 collective-permute-start.2
  562.5 5.1 collective-permute-start.3
  568.4 11.6 %collective-permute-start.4 = (bf16[128,1536]{1,0:T(8,128)(2,1)S(1)}, bf16[128,1536]{1,0:T(8,128)(2,1)S(1)}, u32[]{:S(2)}, u32[]{:S(2)}) collective-permute-start(bf16[128,1536]{1,0:T(8,128)(2,1)S(1)} %multiply_convert_fusion.10), channel_id=1, source_target_pairs={{0,32},{32,64},{64,96},{96,128},{128,160},{160,192},{192,224},{224... | collective-permute-start | bytes 1179656 | tf_op jit(solution)/shard_map/while/body/eval_jaxpr/ppermute | solution.py:30
  587.5 11.1 %collective-permute-start = (bf16[128,1536]{1,0:T(8,128)(2,1)S(1)}, bf16[128,1536]{1,0:T(8,128)(2,1)S(1)}, u32[]{:S(2)}, u32[]{:S(2)}) collective-permute-start(bf16[128,1536]{1,0:T(8,128)(2,1)S(1)} %slice.284), channel_id=1, source_target_pairs={{2,0},{4,2},{6,4},{8,6},{10,8},{12,10},{14,12},{16,14},{18,16},{20... | collective-permute-start | bytes 1179656 | tf_op jit(solution)/shard_map/while/body/eval_jaxpr/ppermute | solution.py:22
  589.4 10.4 %collective-permute-start.1 = (bf16[128,1536]{1,0:T(8,128)(2,1)S(1)}, bf16[128,1536]{1,0:T(8,128)(2,1)S(1)}, u32[]{:S(2)}, u32[]{:S(2)}) collective-permute-start(bf16[128,1536]{1,0:T(8,128)(2,1)S(1)} %slice.284), channel_id=1, source_target_pairs={{0,2},{2,4},{4,6},{6,8},{8,10},{10,12},{12,14},{14,16},{16,18},{18... | collective-permute-start | bytes 1179656 | tf_op jit(solution)/shard_map/while/body/eval_jaxpr/ppermute | solution.py:19
  605.4 19.7 %copy-start.1 = (bf16[2,128,1536]{2,1,0:T(8,128)(2,1)S(1)}, bf16[2,128,1536]{2,1,0:T(8,128)(2,1)}, u32[]{:S(2)}) copy-start(bf16[2,128,1536]{2,1,0:T(8,128)(2,1)} %get-tuple-element.687) | copy-start | bytes 2359300 | tf_op jit(solution)/shard_map/while
  605.8 6.4 collective-permute-start.2
  607.7 5.1 collective-permute-start.3
  613.5 11.6 %collective-permute-start.4 = (bf16[128,1536]{1,0:T(8,128)(2,1)S(1)}, bf16[128,1536]{1,0:T(8,128)(2,1)S(1)}, u32[]{:S(2)}, u32[]{:S(2)}) collective-permute-start(bf16[128,1536]{1,0:T(8,128)(2,1)S(1)} %multiply_convert_fusion.10), channel_id=1, source_target_pairs={{0,32},{32,64},{64,96},{96,128},{128,160},{160,192},{192,224},{224... | collective-permute-start | bytes 1179656 | tf_op jit(solution)/shard_map/while/body/eval_jaxpr/ppermute | solution.py:30
  632.7 11.1 %collective-permute-start = (bf16[128,1536]{1,0:T(8,128)(2,1)S(1)}, bf16[128,1536]{1,0:T(8,128)(2,1)S(1)}, u32[]{:S(2)}, u32[]{:S(2)}) collective-permute-start(bf16[128,1536]{1,0:T(8,128)(2,1)S(1)} %slice.284), channel_id=1, source_target_pairs={{2,0},{4,2},{6,4},{8,6},{10,8},{12,10},{14,12},{16,14},{18,16},{20... | collective-permute-start | bytes 1179656 | tf_op jit(solution)/shard_map/while/body/eval_jaxpr/ppermute | solution.py:22
  634.6 10.4 %collective-permute-start.1 = (bf16[128,1536]{1,0:T(8,128)(2,1)S(1)}, bf16[128,1536]{1,0:T(8,128)(2,1)S(1)}, u32[]{:S(2)}, u32[]{:S(2)}) collective-permute-start(bf16[128,1536]{1,0:T(8,128)(2,1)S(1)} %slice.284), channel_id=1, source_target_pairs={{0,2},{2,4},{4,6},{6,8},{8,10},{10,12},{12,14},{14,16},{16,18},{18... | collective-permute-start | bytes 1179656 | tf_op jit(solution)/shard_map/while/body/eval_jaxpr/ppermute | solution.py:19
  650.6 19.7 %copy-start.1 = (bf16[2,128,1536]{2,1,0:T(8,128)(2,1)S(1)}, bf16[2,128,1536]{2,1,0:T(8,128)(2,1)}, u32[]{:S(2)}) copy-start(bf16[2,128,1536]{2,1,0:T(8,128)(2,1)} %get-tuple-element.687) | copy-start | bytes 2359300 | tf_op jit(solution)/shard_map/while
  651.0 6.4 collective-permute-start.2
  652.9 5.1 collective-permute-start.3
  658.7 11.6 %collective-permute-start.4 = (bf16[128,1536]{1,0:T(8,128)(2,1)S(1)}, bf16[128,1536]{1,0:T(8,128)(2,1)S(1)}, u32[]{:S(2)}, u32[]{:S(2)}) collective-permute-start(bf16[128,1536]{1,0:T(8,128)(2,1)S(1)} %multiply_convert_fusion.10), channel_id=1, source_target_pairs={{0,32},{32,64},{64,96},{96,128},{128,160},{160,192},{192,224},{224... | collective-permute-start | bytes 1179656 | tf_op jit(solution)/shard_map/while/body/eval_jaxpr/ppermute | solution.py:30
  (14 other events, 18.6 us)
Sparse Core Ops, SparseCore 0:
  10.1 83.0 all-gather.3
  95.9 77.2 all-gather.7
  176.0 93.6 all-gather.5
where the time goes:
time: 684 us; the launch traced here: 678 us
  waiting for transfers between devices  399 us (58%)
  starting transfers between devices  120 us (18%)
  matrix products  96.1 us (14%)
  local copies, waits for them, and re-layouts  25.5 us (4%)
  other arithmetic  22.8 us (3%)
  between operations  13.1 us (2%)
    ppermute x9, waiting for transfers between devices, from_behind(): return lax.ppermute(value, axis, pairs)  103 us
    all_gather x1, waiting for transfers between devices, shards(): lax.all_gather(w_qkv, ('seq', 'dp'), axis=1, tiled=True)  96.5 us
    ppermute x18, starting transfers between devices, extended(): lax.ppermute(lax.slice_in_dim(block, block.shape[dim] - width, None, axis...  84 us
    all_gather x1, waiting for transfers between devices, shards(): lax.all_gather(stem_weight, ('seq', 'dp'), axis=0, tiled=True)  82.9 us
    all_gather x1, waiting for transfers between devices, shards(): lax.all_gather(w_out, ('seq', 'dp'), axis=1, tiled=True)  80 us
    dot_general x9, matrix products, apply_layer(): jnp.dot(normed, full_qkv, preferred_element_type=jnp.float32)  37.7 us
    ppermute x18, starting transfers between devices, extended(): lax.ppermute(lax.slice_in_dim(block, 0, width, axis=dim), axis, backward)  34.8 us
    dot_general x9, matrix products, band_attention(): jnp.einsum('hqk,khd->qhd', probs, value_rows, preferred_element_type=jnp....  19 us
  transfers between devices with their start and end apart: 48, of which 39 were waited for; matrix products, arithmetic and copies ran while one was open for 2% of the time, Pallas kernels for 0%

commit v1 on v0

v1 whole, which is shorter than its diff:
```python
import functools

import jax
import jax.numpy as jnp
from jax import lax
from jax.experimental import pallas as pl
from jax.experimental.pallas import tpu as pltpu
from jax.sharding import PartitionSpec as P

HEADS = 8
STRIDE = 4
CHUNKS = 4
eps = 1e-05
masked_score = -1e30
F32 = jnp.float32
BF16 = jnp.bfloat16
MESH = pl.DeviceIdType.MESH


def remote(src, dst, send, recv, **device):
    return pltpu.make_async_remote_copy(
        src_ref=src, dst_ref=dst, send_sem=send, recv_sem=recv, device_id=device, device_id_type=MESH
    )


def rows(ref, start, count):
    return ref.at[pl.ds(pl.multiple_of(start, 16), count)]


def kernel(
    sections, nseq,
    lengths, grouped, stem_in, qkv_in, out_in, gains, taps, arrivals,
    stem_full, qkv_full, out_full, out_peer, xs, normed, kv, queries, context, mask, stream, conv_in, result,
    local_sem, pair_send, pair_recv, ring_send, ring_recv, cross_send, cross_recv,
    halo_send, halo_recv, rim_send, rim_recv, relay_send, relay_recv, done_sem,
):
    section = lax.axis_index("section")
    seq = lax.axis_index("seq")
    dp = lax.axis_index("dp")
    nz = nseq // 2
    z, core = seq // 2, seq % 2
    ahead = ((z + 1) % nz) * 2 + core
    behind = ((z + nz - 1) % nz) * 2 + core
    other = seq + 1 - 2 * core
    right, left = (seq + 1) % nseq, (seq + nseq - 1) % nseq
    far = jnp.where(core == 1, right, left)
    following, preceding = (section + 1) % sections, (section + sections - 1) % sections
    first = section == 0

    micro, frames, width = xs.shape[0] // 2, xs.shape[1], xs.shape[2]
    heads_width = queries.shape[1]
    head_size = heads_width // HEADS
    stem_rows, qkv_rows, out_rows = stem_in.shape[0], qkv_in.shape[0], out_in.shape[0]

    barrier = pltpu.get_barrier_semaphore()
    for device in (
        {"seq": ahead}, {"seq": behind}, {"seq": other}, {"seq": far},
        {"dp": 1 - dp}, {"section": following}, {"section": preceding},
    ):
        pl.semaphore_signal(barrier, inc=1, device_id=device, device_id_type=MESH)
    pl.semaphore_wait(barrier, 7)

    def own_rows(full, count):
        return rows(full, (seq * 2 + dp) * count, count)

    stem_pair = remote(stem_in, own_rows(stem_full, stem_rows), pair_send.at[2], pair_recv.at[2], dp=1 - dp)
    stem_keep = pltpu.make_async_copy(stem_in, own_rows(stem_full, stem_rows), local_sem.at[1])
    qkv_pair = remote(qkv_in, own_rows(qkv_full, qkv_rows), pair_send.at[0], pair_recv.at[0], dp=1 - dp)
    qkv_keep = pltpu.make_async_copy(qkv_in, own_rows(qkv_full, qkv_rows), local_sem.at[0])
    out_pair = remote(out_in, out_peer, pair_send.at[1], pair_recv.at[1], dp=1 - dp)

    @pl.when(first)
    def _():
        stem_pair.start()
        stem_keep.start()

    qkv_pair.start()
    qkv_keep.start()
    out_pair.start()

    def block(full, count, zz, cc, low=0, high=None):
        high = count if high is None else high
        return rows(full, (zz * 2 + cc) * count + low, high - low)

    steps = nz // 2

    def ring(arrays, beside=None):
        sent = []
        for t in range(steps):
            last = t == steps - 1
            zf, zb = (z + nz - t) % nz, (z + t) % nz
            moves = []
            for index, full, count, cut in arrays:
                src = block(full, count, zf, core, 0, cut if last else count)
                moves.append(remote(src, src, ring_send.at[index, 0, t], ring_recv.at[index, 0, t], seq=ahead))
                src = block(full, count, zb, core, cut if last else 0, count)
                moves.append(remote(src, src, ring_send.at[index, 1, t], ring_recv.at[index, 1, t], seq=behind))
            for move in moves:
                move.start()
            crossing = []
            for index, full, count, cut in arrays:
                src = block(full, count, zf, core)
                crossing.append(remote(src, src, cross_send.at[index, t], cross_recv.at[index, t], seq=other))
                if t > 0:
                    src = block(full, count, zb, core)
                    crossing.append(
                        remote(src, src, cross_send.at[index, steps + t], cross_recv.at[index, steps + t], seq=other)
                    )
            for move in crossing:
                move.start()
            if t == 0 and beside is not None:
                beside()
            for move in moves:
                move.wait_recv()
            sent += moves
            sent += crossing
        crossing = []
        for index, full, count, cut in arrays:
            src = block(full, count, (z + steps) % nz, core)
            crossing.append(remote(src, src, cross_send.at[index, steps], cross_recv.at[index, steps], seq=other))
        for move in crossing:
            move.start()
        for index, full, count, cut in arrays:
            for slot in range(2 * steps):
                src = block(full, count, z, core)
                remote(src, src, cross_send.at[index, slot], cross_recv.at[index, slot], seq=other).wait_recv()
        for move in sent + crossing:
            move.wait_send()

    def positions(shape, dim):
        return lax.broadcasted_iota(jnp.int32, shape, dim)

    def valid_rows(m, start, count):
        return (seq * frames + start + positions((count, 1), 0) < lengths[m]).astype(F32)

    def stem():
        for m in range(micro):
            for start in range(0, width, 256):
                value = jnp.dot(grouped[m], stem_full[:, start : start + 256], preferred_element_type=F32)
                value = value * jax.nn.sigmoid(value) * valid_rows(m, 0, frames)
                xs[micro + m, :, start : start + 256] = value.astype(BF16)

    @pl.when(first)
    def _():
        stem_keep.wait()
        stem_pair.wait()
        ring([(2, stem_full, 2 * stem_rows, stem_rows)])

    qkv_keep.wait()
    qkv_pair.wait()
    out_pair.wait()
    mine, theirs = out_in[...], out_peer[...]
    both = jnp.concatenate(
        [jnp.where(dp == 0, mine, theirs), jnp.where(dp == 0, theirs, mine)], axis=0
    )
    out_full[pl.ds(pl.multiple_of(seq * 2 * out_rows, 16), 2 * out_rows)] = both

    def beside():
        @pl.when(first)
        def _():
            stem()

    ring(
        [(0, qkv_full, 2 * qkv_rows, qkv_rows), (1, out_full, 2 * out_rows, (2 * out_rows) // 32 * 16 + 16 * ((2 * out_rows) // 16 % 2))],
        beside,
    )

    per_chunk = frames // CHUNKS

    def relay(m, c):
        start = c * per_chunk
        return remote(
            result.at[m, pl.ds(start, per_chunk)], xs.at[m, pl.ds(start, per_chunk)],
            relay_send.at[m, c], relay_recv.at[m, c], section=following,
        )

    def halo(m, part, side):
        columns = pl.ds(part * heads_width, heads_width)
        src = kv.at[m, pl.ds(frames, frames), columns]
        dst = kv.at[m, pl.ds(0 if side == 0 else 2 * frames, frames), columns]
        return remote(
            src, dst, halo_send.at[m, part, side], halo_recv.at[m, part, side], seq=right if side == 0 else left
        )

    def rim(m, side):
        src = conv_in.at[m, pl.ds(frames if side == 0 else 8, 8)]
        dst = conv_in.at[m, pl.ds(0 if side == 0 else 8 + frames, 8)]
        return remote(src, dst, rim_send.at[m, side], rim_recv.at[m, side], seq=right if side == 0 else left)

    def keep(m):
        return pltpu.make_async_copy(xs.at[m], arrivals.at[m], done_sem.at[m])

    def norm(value, gain):
        average = jnp.mean(value, axis=-1, keepdims=True)
        centered = value - average
        variance = jnp.mean(centered * centered, axis=-1, keepdims=True)
        return centered * lax.rsqrt(variance + eps) * gain

    def layer(m, carry):
        length = lengths[m]
        span = 3 * frames
        query = positions((frames, span), 0)
        key = positions((frames, span), 1)
        place = seq * frames - frames + key
        allowed = (place >= 0) & (place < length) & (key >= query) & (key <= query + 2 * frames)
        mask[...] = jnp.where(allowed, 0.0, masked_score).astype(F32)

        @pl.when(jnp.logical_not(first))
        def _():
            for c in range(CHUNKS):
                relay(m, c).wait_recv()
            keep(m).start()

        slot = jnp.where(first, micro + m, m)
        for start in range(0, frames, 16):
            value = xs[slot, start : start + 16, :].astype(F32)
            normed[start : start + 16, :] = norm(value, gains[0:1, :]).astype(BF16)

        for part in range(2):
            for start in range(0, heads_width, 256):
                at = heads_width * (1 + part) + start
                value = jnp.dot(normed[...], qkv_full[:, at : at + 256], preferred_element_type=F32)
                at = heads_width * part + start
                kv[m, frames : 2 * frames, at : at + 256] = value.astype(BF16)
            halo(m, part, 0).start()
            halo(m, part, 1).start()
        for start in range(0, heads_width, 256):
            value = jnp.dot(normed[...], qkv_full[:, start : start + 256], preferred_element_type=F32)
            queries[:, start : start + 256] = value.astype(BF16)
        for part in range(2):
            halo(m, part, 0).wait_recv()
            halo(m, part, 1).wait_recv()

        scale = 1.0 / head_size**0.5
        for group in range(HEADS // 4):
            base = group * 4 * head_size
            outs = []
            for h in range(4):
                low, high = h * head_size, (h + 1) * head_size
                lane_low, lane_high = low // 128 * 128, -(-high // 128) * 128
                lane = positions((frames, lane_high - lane_low), 1) + lane_low
                q = queries[:, base + lane_low : base + lane_high]
                q = jnp.where((lane >= low) & (lane < high), q, jnp.zeros_like(q))
                k = kv[m, :, base + lane_low : base + lane_high]
                v = kv[m, :, heads_width + base + lane_low : heads_width + base + lane_high]
                scores = lax.dot_general(q, k, (((1,), (1,)), ((), ())), preferred_element_type=F32)
                scores = scores * scale + mask[...]
                highest = jnp.max(scores, axis=-1, keepdims=True)
                expon = jnp.exp(scores - highest)
                total = jnp.sum(expon, axis=-1, keepdims=True)
                probs = (expon * (1.0 / total)).astype(BF16)
                outs.append(jnp.dot(probs, v, preferred_element_type=F32))
            lane = positions((frames, 128), 1)
            tiles = [
                jnp.where(lane < 96, outs[0], outs[1][:, :128]),
                jnp.where(lane < 64, outs[1][:, 128:], outs[2][:, :128]),
                jnp.where(lane < 32, outs[2][:, 128:], outs[3]),
            ]
            for index, tile in enumerate(tiles):
                at = base + index * 128
                context[:, at : at + 128] = tile.astype(BF16)

        for start in range(0, width, 256):
            value = jnp.dot(context[...], out_full[:, start : start + 256], preferred_element_type=F32)
            stream[:, start : start + 256] = value + xs[slot, :, start : start + 256].astype(F32)

        for start in range(0, frames, 16):
            value = norm(stream[start : start + 16, :], gains[1:2, :]) * valid_rows(m, start, 16)
            conv_in[m, 8 + start : 8 + start + 16, :] = value.astype(BF16).astype(F32)
        for side in range(2):
            rim(m, side).start()
        for side in range(2):
            rim(m, side).wait_recv()
        conv_in[m, 0:8, :] = jnp.where(seq == 0, 0.0, conv_in[m, 0:8, :])
        conv_in[m, 8 + frames : 16 + frames, :] = jnp.where(seq == nseq - 1, 0.0, conv_in[m, 8 + frames : 16 + frames, :])

        count = taps.shape[0]
        for c in range(CHUNKS):
            for start in range(c * per_chunk, (c + 1) * per_chunk, 16):
                conv = jnp.zeros((16, width), F32)
                for offset in range(count):
                    at = 8 - count // 2 + start + offset
                    conv = conv + conv_in[m, at : at + 16, :] * taps[offset : offset + 1, :]
                value = (stream[start : start + 16, :] + conv * jax.nn.sigmoid(conv)) * valid_rows(m, start, 16)
                result[m, start : start + 16, :] = value.astype(BF16)
            relay(m, c).start()
        return carry

    lax.fori_loop(0, micro, layer, 0)

    @pl.when(first)
    def _():
        for m in range(micro):
            for c in range(CHUNKS):
                relay(m, c).wait_recv()
            keep(m).start()

    for m in range(micro):
        for c in range(CHUNKS):
            relay(m, c).wait_send()
        for side in range(2):
            rim(m, side).wait_send()
            for part in range(2):
                halo(m, part, side).wait_send()
        keep(m).wait()


def shards(sections, nseq, mel, lengths, stem_weight, w_qkv, w_out, norm_gains, conv_kernel):
    micro = mel.shape[0]
    frames = mel.shape[1] // STRIDE
    width = stem_weight.shape[1]
    heads_width = w_qkv.shape[2] // 3
    grouped = mel.reshape(micro, frames, STRIDE * mel.shape[2])
    depth, full_out = w_qkv.shape[1] * 2 * nseq, w_out.shape[1] * 2 * nseq
    steps = nseq // 4
    dma = pltpu.SemaphoreType.DMA
    vmem = pl.BlockSpec(memory_space=pltpu.VMEM)
    arrived = pl.pallas_call(
        functools.partial(kernel, sections, nseq),
        out_shape=jax.ShapeDtypeStruct((micro, frames, width), BF16),
        in_specs=[pl.BlockSpec(memory_space=pltpu.SMEM)] + [vmem] * 6,
        out_specs=pl.BlockSpec(memory_space=pl.ANY),
        scratch_shapes=[
            pltpu.VMEM((stem_weight.shape[0] * 2 * nseq, width), BF16),
            pltpu.VMEM((depth, 3 * heads_width), BF16),
            pltpu.VMEM((full_out, width), BF16),
            pltpu.VMEM(w_out.shape[1:], BF16),
            pltpu.VMEM((2 * micro, frames, width), BF16),
            pltpu.VMEM((frames, width), BF16),
            pltpu.VMEM((micro, 3 * frames, 2 * heads_width), BF16),
            pltpu.VMEM((frames, heads_width), BF16),
            pltpu.VMEM((frames, heads_width), BF16),
            pltpu.VMEM((frames, 3 * frames), F32),
            pltpu.VMEM((frames, width), F32),
            pltpu.VMEM((micro, frames + 16, width), F32),
            pltpu.VMEM((micro, frames, width), BF16),
            dma((2,)),
            dma((3,)),
            dma((3,)),
            dma((3, 2, steps)),
            dma((3, 2, steps)),
            dma((3, 2 * steps)),
            dma((3, 2 * steps)),
            dma((micro, 2, 2)),
            dma((micro, 2, 2)),
            dma((micro, 2)),
            dma((micro, 2)),
            dma((micro, CHUNKS)),
            dma((micro, CHUNKS)),
            dma((micro,)),
        ],
        compiler_params=pltpu.CompilerParams(
            collective_id=0, has_side_effects=True, vmem_limit_bytes=48 * 1024 * 1024
        ),
    )(lengths, grouped, stem_weight, w_qkv[0], w_out[0], norm_gains[0], conv_kernel[0])
    return arrived[None]


def solution(mesh):
    return jax.shard_map(
        functools.partial(shards, mesh.shape["section"], mesh.shape["seq"]),
        mesh=mesh,
        in_specs=(
            P("dp", "seq", None),
            P("dp"),
            P(("seq", "dp"), None),
            P("section", ("seq", "dp"), None),
            P("section", ("seq", "dp"), None),
            P("section", None, None),
            P("section", None, None),
        ),
        out_specs=P("section", "dp", "seq", None),
        check_vma=False,
    )
```

time: 684 us -> 298 us (0.44)
  waiting for transfers between devices: 399 us -> 0 us
  Pallas kernels: 0 us -> 293 us
  starting transfers between devices: 120 us -> 0 us
  matrix products: 96.1 us -> 0 us
  other arithmetic: 22.8 us -> 0 us
  local copies, waits for them, and re-layouts: 25.5 us -> 2.85 us
  between operations: 13.1 us -> 0.08 us
    pallas_call x0 -> x1, Pallas kernels: none -> 293 us  [shards(): pl.pallas_call(functools.partial(kernel, sections, nseq), out_shape=jax.S...]
    all_gather x3 -> x0, waiting for transfers between devices: 259 us -> none  [the longest x1 96.5 us: shards(): lax.all_gather(w_qkv, ('seq', 'dp'), axis=1, tiled=True)]
    ppermute x45 -> x0, waiting for transfers between devices: 137 us -> none  [the longest x9 103 us: from_behind(): return lax.ppermute(value, axis, pairs)]
    ppermute x45 -> x0, starting transfers between devices: 120 us -> none  [the longest x18 84 us: extended(): lax.ppermute(lax.slice_in_dim(block, block.shape[dim] - width, None, axis...]
    dot_general x36 -> x0, matrix products: 79.3 us -> none  [the longest x9 37.7 us: apply_layer(): jnp.dot(normed, full_qkv, preferred_element_type=jnp.float32)]
    sub x9 -> x0, matrix products: 16.7 us -> none  [band_attention(): expon = jnp.exp(scores - highest)]
    convert_element_type x19 -> x0, other arithmetic: 9.69 us -> none  [the longest x9 6.2 us: apply_layer(): return ((stream + jax.nn.silu(conv)) * valid[:, None]).astype(jnp.bfloat16)]
    slice x81 -> x0, local copies, waits for them, and re-layouts: 9.27 us -> none  [the longest x18 3.44 us: band_attention(): key_rows = keys_values[:, :width].reshape(span, heads, head_size)]
  transfers between devices with their start and end apart: 48 -> 0, of which waited for: 39 -> 0; matrix products, arithmetic and copies ran while one was open for 2% -> 0% of each run, Pallas kernels for 0% -> 0%
where the time goes in v1:
time: 298 us; the launch traced here: 296 us
  Pallas kernels  293 us (98%)
    pallas_call x1, Pallas kernels, shards(): pl.pallas_call(functools.partial(kernel, sections, nseq), out_shape=jax.S...  293 us

profile of v1, /device:TPU:1, one launch (start us, length us, event | category | flops | bytes accessed | tf_op | source)
XLA Modules:
  0.0 296.2 jit_solution(9314662677759146286)
XLA Ops:
  0.0 0.8 copy.10
  0.8 0.0 copy-start
  0.8 0.0 copy-start.1
  0.8 0.0 copy-start.2
  0.8 0.0 copy-start.3
  0.8 0.0 copy-start.4
  0.8 1.2 reshape.3.grouped
  2.0 0.0 copy-done
  2.0 0.0 copy-done.1
  2.0 0.0 copy-done.2
  2.0 0.0 copy-done.3
  2.0 0.0 copy-done.4
  2.0 293.3 %shard_map.73 = bf16[2,128,1536]{2,1,0:T(8,128)(2,1)S(1)} custom-call(s32[2]{0:T(128)S(1)} %copy-done.4, bf16[2,128,512]{2,1,0:T(8,128)(2,1)S(1)} %reshape.3.grouped, bf16[16,1536]{1,0:T(8,128)(2,1)S(1)} %copy-done.2, bf16[48,2304]{1,0:T(8,128)(2,1)S(1)} %bitcast.8, bf16[24,1536]{1,0:T(8,128)(2,1)S(1)} %bitcast.10, f32[2,1536]{1,0:T(2,128)S(1)} %bitcast.11, ...), custom_call_target="tpu_custom_call" | custom-call | tf_op jit(solution)/shard_map/pallas_call | solution.py:318
  295.4 0.9 copy.12
Async XLA Ops:
  0.8 1.2 copy-start
  0.8 1.2 copy-start.1
  0.8 1.2 copy-start.2
  0.8 1.2 copy-start.3
  0.8 1.2 copy-start.4

commit v2 on v1

--- a/solution.py
+++ b/solution.py
@@ -9,7 +9,6 @@
 
 HEADS = 8
 STRIDE = 4
-CHUNKS = 4
 eps = 1e-05
 masked_score = -1e30
 F32 = jnp.float32
@@ -38,13 +37,13 @@
     seq = lax.axis_index("seq")
     dp = lax.axis_index("dp")
     nz = nseq // 2
-    z, core = seq // 2, seq % 2
-    ahead = ((z + 1) % nz) * 2 + core
-    behind = ((z + nz - 1) % nz) * 2 + core
+    z, core = lax.div(seq, 2), lax.rem(seq, 2)
+    ahead = lax.rem(z + 1, nz) * 2 + core
+    behind = lax.rem(z + nz - 1, nz) * 2 + core
     other = seq + 1 - 2 * core
-    right, left = (seq + 1) % nseq, (seq + nseq - 1) % nseq
+    right, left = lax.rem(seq + 1, nseq), lax.rem(seq + nseq - 1, nseq)
     far = jnp.where(core == 1, right, left)
-    following, preceding = (section + 1) % sections, (section + sections - 1) % sections
+    following, preceding = lax.rem(section + 1, sections), lax.rem(section + sections - 1, sections)
     first = section == 0
 
     micro, frames, width = xs.shape[0] // 2, xs.shape[1], xs.shape[2]
@@ -78,60 +77,79 @@
     qkv_keep.start()
     out_pair.start()
 
-    def block(full, count, zz, cc, low=0, high=None):
-        high = count if high is None else high
-        return rows(full, (zz * 2 + cc) * count + low, high - low)
-
     steps = nz // 2
 
-    def ring(arrays, beside=None):
-        sent = []
+    places = [
+        [(lax.rem(z + nz - t, nz) * 2 + core) for t in range(steps + 1)],
+        [(lax.rem(z + t, nz) * 2 + core) for t in range(steps)],
+    ]
+    out_cut = -(-out_rows // 16) * 16
+    arrays = {
+        "stem": (0, stem_full, stem_rows, 0, 2 * stem_rows, stem_rows),
+        "own": (1, qkv_full, qkv_rows, dp * qkv_rows, qkv_rows, qkv_rows),
+        "peer": (2, qkv_full, qkv_rows, (1 - dp) * qkv_rows, qkv_rows, 0),
+        "out": (3, out_full, out_rows, 0, 2 * out_rows, out_cut),
+    }
+    hops, crosses = {}, {}
+    for name, (index, full, count, low, size, cut) in arrays.items():
+        for side in range(2):
+            for t in range(steps):
+                start, length = places[side][t] * (2 * count) + low, size
+                if t == steps - 1:
+                    start, length = (start, cut) if side == 0 else (start + cut, size - cut)
+                if length:
+                    src = rows(full, start, length)
+                    hops[name, side, t] = remote(
+                        src, src, ring_send.at[index, side, t], ring_recv.at[index, side, t],
+                        seq=ahead if side == 0 else behind,
+                    )
+        for slot in range(2 * steps):
+            place = places[0][slot] if slot <= steps else places[1][slot - steps]
+            src = rows(full, place * (2 * count) + low, size)
+            crosses[name, slot] = remote(src, src, cross_send.at[index, slot], cross_recv.at[index, slot], seq=other)
+
+    def hop(name, side, t):
+        return hops.get((name, side, t))
+
+    def cross(name, slot):
+        return crosses[name, slot]
+
+    def ring_open(name):
+        for side in range(2):
+            hop(name, side, 0).start()
+        cross(name, 0).start()
+
+    def ring_step(name, t):
+        for side in range(2):
+            hop(name, side, t - 1).wait_recv()
+            move = hop(name, side, t)
+            if move is not None:
+                move.start()
+            cross(name, t if side == 0 else steps + t).start()
+
+    def ring_close(name):
+        for side in range(2):
+            move = hop(name, side, steps - 1)
+            if move is not None:
+                move.wait_recv()
+        cross(name, steps).start()
+        for slot in range(2 * steps):
+            cross(name, slot).wait_recv()
+
+    def ring_sent(name):
         for t in range(steps):
-            last = t == steps - 1
-            zf, zb = (z + nz - t) % nz, (z + t) % nz
-            moves = []
-            for index, full, count, cut in arrays:
-                src = block(full, count, zf, core, 0, cut if last else count)
-                moves.append(remote(src, src, ring_send.at[index, 0, t], ring_recv.at[index, 0, t], seq=ahead))
-                src = block(full, count, zb, core, cut if last else 0, count)
-                moves.append(remote(src, src, ring_send.at[index, 1, t], ring_recv.at[index, 1, t], seq=behind))
-            for move in moves:
-                move.start()
-            crossing = []
-            for index, full, count, cut in arrays:
-                src = block(full, count, zf, core)
-                crossing.append(remote(src, src, cross_send.at[index, t], cross_recv.at[index, t], seq=other))
-                if t > 0:
-                    src = block(full, count, zb, core)
-                    crossing.append(
-                        remote(src, src, cross_send.at[index, steps + t], cross_recv.at[index, steps + t], seq=other)
-                    )
-            for move in crossing:
-                move.start()
-            if t == 0 and beside is not None:
-                beside()
-            for move in moves:
-                move.wait_recv()
-            sent += moves
-            sent += crossing
-        crossing = []
-        for index, full, count, cut in arrays:
-            src = block(full, count, (z + steps) % nz, core)
-            crossing.append(remote(src, src, cross_send.at[index, steps], cross_recv.at[index, steps], seq=other))
-        for move in crossing:
-            move.start()
-        for index, full, count, cut in arrays:
-            for slot in range(2 * steps):
-                src = block(full, count, z, core)
-                remote(src, src, cross_send.at[index, slot], cross_recv.at[index, slot], seq=other).wait_recv()
-        for move in sent + crossing:
-            move.wait_send()
+            for side in range(2):
+                move = hop(name, side, t)
+                if move is not None:
+                    move.wait_send()
+        for slot in range(2 * steps):
+            cross(name, slot).wait_send()
 
     def positions(shape, dim):
         return lax.broadcasted_iota(jnp.int32, shape, dim)
 
     def valid_rows(m, start, count):
-        return (seq * frames + start + positions((count, 1), 0) < lengths[m]).astype(F32)
+        return jnp.where(positions((count, 1), 0) < lengths[m] - seq * frames - start, 1.0, 0.0)
 
     def stem():
         for m in range(micro):
@@ -140,46 +158,57 @@
                 value = value * jax.nn.sigmoid(value) * valid_rows(m, 0, frames)
                 xs[micro + m, :, start : start + 256] = value.astype(BF16)
 
+    qkv_keep.wait()
+    ring_open("own")
+
     @pl.when(first)
     def _():
         stem_keep.wait()
         stem_pair.wait()
-        ring([(2, stem_full, 2 * stem_rows, stem_rows)])
-
-    qkv_keep.wait()
+        ring_open("stem")
+
     qkv_pair.wait()
+    ring_open("peer")
     out_pair.wait()
     mine, theirs = out_in[...], out_peer[...]
     both = jnp.concatenate(
         [jnp.where(dp == 0, mine, theirs), jnp.where(dp == 0, theirs, mine)], axis=0
     )
     out_full[pl.ds(pl.multiple_of(seq * 2 * out_rows, 16), 2 * out_rows)] = both
-
-    def beside():
+    ring_open("out")
+    for t in range(1, steps):
         @pl.when(first)
         def _():
-            stem()
-
-    ring(
-        [(0, qkv_full, 2 * qkv_rows, qkv_rows), (1, out_full, 2 * out_rows, (2 * out_rows) // 32 * 16 + 16 * ((2 * out_rows) // 16 % 2))],
-        beside,
-    )
-
-    per_chunk = frames // CHUNKS
-
-    def relay(m, c):
-        start = c * per_chunk
+            ring_step("stem", t)
+
+        for name in ("own", "peer", "out"):
+            ring_step(name, t)
+
+    @pl.when(first)
+    def _():
+        ring_close("stem")
+        stem()
+        ring_sent("stem")
+
+    ring_close("own")
+    ring_close("peer")
+
+    units = ((16, frames // 2 - 16), (frames // 2, frames // 2 - 16), (0, 16), (frames - 16, 16))
+    groups = ((0,), (1,), (2, 3))
+
+    def relay(m, unit):
+        start, count = units[unit]
         return remote(
-            result.at[m, pl.ds(start, per_chunk)], xs.at[m, pl.ds(start, per_chunk)],
-            relay_send.at[m, c], relay_recv.at[m, c], section=following,
+            result.at[m, pl.ds(start, count)], xs.at[m, pl.ds(start, count)],
+            relay_send.at[m, unit], relay_recv.at[m, unit], section=following,
         )
 
-    def halo(m, part, side):
-        columns = pl.ds(part * heads_width, heads_width)
-        src = kv.at[m, pl.ds(frames, frames), columns]
-        dst = kv.at[m, pl.ds(0 if side == 0 else 2 * frames, frames), columns]
+    def halo(m, unit, side):
+        start, count = units[unit]
+        src = kv.at[m, pl.ds(frames + start, count)]
+        dst = kv.at[m, pl.ds(start if side == 0 else 2 * frames + start, count)]
         return remote(
-            src, dst, halo_send.at[m, part, side], halo_recv.at[m, part, side], seq=right if side == 0 else left
+            src, dst, halo_send.at[m, unit, side], halo_recv.at[m, unit, side], seq=right if side == 0 else left
         )
 
     def rim(m, side):
@@ -205,31 +234,41 @@
         allowed = (place >= 0) & (place < length) & (key >= query) & (key <= query + 2 * frames)
         mask[...] = jnp.where(allowed, 0.0, masked_score).astype(F32)
 
+        slot = jnp.where(first, micro + m, m)
+        for group in groups:
+            @pl.when(jnp.logical_not(first))
+            def _():
+                for unit in group:
+                    relay(m, unit).wait_recv()
+
+            for unit in group:
+                for start in range(units[unit][0], sum(units[unit]), 16):
+                    value = xs[slot, start : start + 16, :].astype(F32)
+                    normed[start : start + 16, :] = norm(value, gains[0:1, :]).astype(BF16)
+            some = [normed[units[unit][0] : sum(units[unit]), :] for unit in group]
+            some = some[0] if len(some) == 1 else jnp.concatenate(some, axis=0)
+            for start in range(0, 2 * heads_width, 256):
+                at = heads_width + start
+                value = jnp.dot(some, qkv_full[:, at : at + 256], preferred_element_type=F32).astype(BF16)
+                low = 0
+                for unit in group:
+                    at, count = units[unit]
+                    kv[m, frames + at : frames + at + count, start : start + 256] = value[low : low + count]
+                    low += count
+            for unit in group:
+                for side in range(2):
+                    halo(m, unit, side).start()
+
         @pl.when(jnp.logical_not(first))
         def _():
-            for c in range(CHUNKS):
-                relay(m, c).wait_recv()
             keep(m).start()
 
-        slot = jnp.where(first, micro + m, m)
-        for start in range(0, frames, 16):
-            value = xs[slot, start : start + 16, :].astype(F32)
-            normed[start : start + 16, :] = norm(value, gains[0:1, :]).astype(BF16)
-
-        for part in range(2):
-            for start in range(0, heads_width, 256):
-                at = heads_width * (1 + part) + start
-                value = jnp.dot(normed[...], qkv_full[:, at : at + 256], preferred_element_type=F32)
-                at = heads_width * part + start
-                kv[m, frames : 2 * frames, at : at + 256] = value.astype(BF16)
-            halo(m, part, 0).start()
-            halo(m, part, 1).start()
         for start in range(0, heads_width, 256):
             value = jnp.dot(normed[...], qkv_full[:, start : start + 256], preferred_element_type=F32)
             queries[:, start : start + 256] = value.astype(BF16)
-        for part in range(2):
-            halo(m, part, 0).wait_recv()
-            halo(m, part, 1).wait_recv()
+        for unit in range(len(units)):
+            for side in range(2):
+                halo(m, unit, side).wait_recv()
 
         scale = 1.0 / head_size**0.5
         for group in range(HEADS // 4):
@@ -260,6 +299,10 @@
                 at = base + index * 128
                 context[:, at : at + 128] = tile.astype(BF16)
 
+        @pl.when(m == 0)
+        def _():
+            ring_close("out")
+
         for start in range(0, width, 256):
             value = jnp.dot(context[...], out_full[:, start : start + 256], preferred_element_type=F32)
             stream[:, start : start + 256] = value + xs[slot, :, start : start + 256].astype(F32)
@@ -269,21 +312,22 @@
             conv_in[m, 8 + start : 8 + start + 16, :] = value.astype(BF16).astype(F32)
         for side in range(2):
             rim(m, side).start()
-        for side in range(2):
-            rim(m, side).wait_recv()
-        conv_in[m, 0:8, :] = jnp.where(seq == 0, 0.0, conv_in[m, 0:8, :])
-        conv_in[m, 8 + frames : 16 + frames, :] = jnp.where(seq == nseq - 1, 0.0, conv_in[m, 8 + frames : 16 + frames, :])
-
         count = taps.shape[0]
-        for c in range(CHUNKS):
-            for start in range(c * per_chunk, (c + 1) * per_chunk, 16):
+        for unit in range(len(units)):
+            if unit == 2:
+                for side in range(2):
+                    rim(m, side).wait_recv()
+                top, bottom = conv_in[m, 0:8, :], conv_in[m, 8 + frames : 16 + frames, :]
+                conv_in[m, 0:8, :] = jnp.where(seq == 0, 0.0, top)
+                conv_in[m, 8 + frames : 16 + frames, :] = jnp.where(seq == nseq - 1, 0.0, bottom)
+            for start in range(units[unit][0], sum(units[unit]), 16):
                 conv = jnp.zeros((16, width), F32)
                 for offset in range(count):
                     at = 8 - count // 2 + start + offset
                     conv = conv + conv_in[m, at : at + 16, :] * taps[offset : offset + 1, :]
                 value = (stream[start : start + 16, :] + conv * jax.nn.sigmoid(conv)) * valid_rows(m, start, 16)
                 result[m, start : start + 16, :] = value.astype(BF16)
-            relay(m, c).start()
+            relay(m, unit).start()
         return carry
 
     lax.fori_loop(0, micro, layer, 0)
@@ -291,17 +335,19 @@
     @pl.when(first)
     def _():
         for m in range(micro):
-            for c in range(CHUNKS):
-                relay(m, c).wait_recv()
+            for unit in range(len(units)):
+                relay(m, unit).wait_recv()
             keep(m).start()
 
+    for name in ("own", "peer", "out"):
+        ring_sent(name)
     for m in range(micro):
-        for c in range(CHUNKS):
-            relay(m, c).wait_send()
+        for unit in range(len(units)):
+            relay(m, unit).wait_send()
+            for side in range(2):
+                halo(m, unit, side).wait_send()
         for side in range(2):
             rim(m, side).wait_send()
-            for part in range(2):
-                halo(m, part, side).wait_send()
         keep(m).wait()
 
 
@@ -337,16 +383,16 @@
             dma((2,)),
             dma((3,)),
             dma((3,)),
-            dma((3, 2, steps)),
-            dma((3, 2, steps)),
-            dma((3, 2 * steps)),
-            dma((3, 2 * steps)),
-            dma((micro, 2, 2)),
-            dma((micro, 2, 2)),
+            dma((4, 2, steps)),
+            dma((4, 2, steps)),
+            dma((4, 2 * steps)),
+            dma((4, 2 * steps)),
+            dma((micro, 4, 2)),
+            dma((micro, 4, 2)),
             dma((micro, 2)),
             dma((micro, 2)),
-            dma((micro, CHUNKS)),
-            dma((micro, CHUNKS)),
+            dma((micro, 4)),
+            dma((micro, 4)),
             dma((micro,)),
         ],
         compiler_params=pltpu.CompilerParams(

time: 298 us -> 245 us (0.82)
  Pallas kernels: 293 us -> 242 us
    pallas_call x1, Pallas kernels: 293 us -> 242 us  [shards(): pl.pallas_call(functools.partial(kernel, sections, nseq), out_shape=jax.S...]
where the time goes in v2:
time: 245 us
  Pallas kernels  242 us (99%)
  local copies, waits for them, and re-layouts  2.85 us (1%)
    pallas_call x1, Pallas kernels, shards(): pl.pallas_call(functools.partial(kernel, sections, nseq), out_shape=jax.S...  242 us

profile of v2, /device:TPU:1, one launch (start us, length us, event | category | flops | bytes accessed | tf_op | source)
XLA Modules:
  0.0 244.5 jit_solution(1771101176745481272)
XLA Ops:
  0.0 0.8 copy.10
  0.8 0.0 copy-start
  0.8 0.0 copy-start.1
  0.8 0.0 copy-start.2
  0.8 0.0 copy-start.3
  0.8 0.0 copy-start.4
  0.8 1.2 reshape.3.grouped
  2.0 0.0 copy-done
  2.0 0.0 copy-done.1
  2.0 0.0 copy-done.2
  2.0 0.0 copy-done.3
  2.0 0.0 copy-done.4
  2.0 241.6 %shard_map.73 = bf16[2,128,1536]{2,1,0:T(8,128)(2,1)S(1)} custom-call(s32[2]{0:T(128)S(1)} %copy-done.4, bf16[2,128,512]{2,1,0:T(8,128)(2,1)S(1)} %reshape.3.grouped, bf16[16,1536]{1,0:T(8,128)(2,1)S(1)} %copy-done.2, bf16[48,2304]{1,0:T(8,128)(2,1)S(1)} %bitcast.8, bf16[24,1536]{1,0:T(8,128)(2,1)S(1)} %bitcast.10, f32[2,1536]{1,0:T(2,128)S(1)} %bitcast.11, ...), custom_call_target="tpu_custom_call" | custom-call | tf_op jit(solution)/shard_map/pallas_call | solution.py:364
  243.6 0.9 copy.12
Async XLA Ops:
  0.8 1.2 copy-start
  0.8 1.2 copy-start.1
  0.8 1.2 copy-start.2
  0.8 1.2 copy-start.3
  0.8 1.2 copy-start.4

commit v3 on v2

--- a/solution.py
+++ b/solution.py
@@ -29,8 +29,8 @@
 def kernel(
     sections, nseq,
     lengths, grouped, stem_in, qkv_in, out_in, gains, taps, arrivals,
-    stem_full, qkv_full, out_full, out_peer, xs, normed, kv, queries, context, mask, stream, conv_in, result,
-    local_sem, pair_send, pair_recv, ring_send, ring_recv, cross_send, cross_recv,
+    stem_full, qkv_full, out_full, out_peer, xs, normed, kv, queries, context, mask, scores, stream, conv_in, result,
+    local_sem, pair_send, pair_recv, ring_send, ring_recv, cross_send, cross_recv, pass_send, pass_recv,
     halo_send, halo_recv, rim_send, rim_recv, relay_send, relay_recv, done_sem,
 ):
     section = lax.axis_index("section")
@@ -83,17 +83,17 @@
         [(lax.rem(z + nz - t, nz) * 2 + core) for t in range(steps + 1)],
         [(lax.rem(z + t, nz) * 2 + core) for t in range(steps)],
     ]
-    out_cut = -(-out_rows // 16) * 16
+    out_cut = out_rows // 16 * 16
     arrays = {
         "stem": (0, stem_full, stem_rows, 0, 2 * stem_rows, stem_rows),
         "own": (1, qkv_full, qkv_rows, dp * qkv_rows, qkv_rows, qkv_rows),
-        "peer": (2, qkv_full, qkv_rows, (1 - dp) * qkv_rows, qkv_rows, 0),
+        "peer": (2, qkv_full, qkv_rows, (1 - dp) * qkv_rows, qkv_rows, qkv_rows),
         "out": (3, out_full, out_rows, 0, 2 * out_rows, out_cut),
     }
-    hops, crosses = {}, {}
+    hops, crosses, pairs = {}, {}, {}
     for name, (index, full, count, low, size, cut) in arrays.items():
         for side in range(2):
-            for t in range(steps):
+            for t in range(1 if name == "peer" else steps):
                 start, length = places[side][t] * (2 * count) + low, size
                 if t == steps - 1:
                     start, length = (start, cut) if side == 0 else (start + cut, size - cut)
@@ -107,6 +107,8 @@
             place = places[0][slot] if slot <= steps else places[1][slot - steps]
             src = rows(full, place * (2 * count) + low, size)
             crosses[name, slot] = remote(src, src, cross_send.at[index, slot], cross_recv.at[index, slot], seq=other)
+            if name == "own" and slot not in (0, 1, steps + 1):
+                pairs[slot] = remote(src, src, pass_send.at[slot], pass_recv.at[slot], dp=1 - dp)
 
     def hop(name, side, t):
         return hops.get((name, side, t))
@@ -121,18 +123,28 @@
 
     def ring_step(name, t):
         for side in range(2):
+            slot = t if side == 0 else steps + t
             hop(name, side, t - 1).wait_recv()
             move = hop(name, side, t)
             if move is not None:
                 move.start()
-            cross(name, t if side == 0 else steps + t).start()
+            cross(name, slot).start()
+            if name == "own" and slot in pairs:
+                pairs[slot].start()
 
     def ring_close(name):
         for side in range(2):
             move = hop(name, side, steps - 1)
             if move is not None:
                 move.wait_recv()
-        cross(name, steps).start()
+        if name == "own":
+            pairs[steps].start()
+        if name != "peer":
+            cross(name, steps).start()
+        for slot in range(2 * steps):
+            if name == "peer" and slot in pairs:
+                pairs[slot].wait_recv()
+                cross(name, slot).start()
         for slot in range(2 * steps):
             cross(name, slot).wait_recv()
 
@@ -144,6 +156,8 @@
                     move.wait_send()
         for slot in range(2 * steps):
             cross(name, slot).wait_send()
+            if name == "own" and slot in pairs:
+                pairs[slot].wait_send()
 
     def positions(shape, dim):
         return lax.broadcasted_iota(jnp.int32, shape, dim)
@@ -181,7 +195,7 @@
         def _():
             ring_step("stem", t)
 
-        for name in ("own", "peer", "out"):
+        for name in ("own", "peer", "out") if t == 1 else ("own", "out"):
             ring_step(name, t)
 
     @pl.when(first)
@@ -206,10 +220,20 @@
     def halo(m, unit, side):
         start, count = units[unit]
         src = kv.at[m, pl.ds(frames + start, count)]
-        dst = kv.at[m, pl.ds(start if side == 0 else 2 * frames + start, count)]
+        dst = kv.at[m, pl.ds(2 * frames * side + start, count)]
         return remote(
             src, dst, halo_send.at[m, unit, side], halo_recv.at[m, unit, side], seq=right if side == 0 else left
         )
+
+    near_side, far_side = 1 - core, core
+    near_keys = pl.multiple_of(frames * (1 - core), 128)
+    far_keys = pl.multiple_of(2 * frames * core, 128)
+
+    def halo_wait(m, side):
+        for unit, (start, count) in enumerate(units):
+            src = kv.at[m, pl.ds(frames + start, count)]
+            dst = rows(kv.at[m], 2 * frames * side + start, count)
+            remote(src, dst, halo_send.at[m, unit, side], halo_recv.at[m, unit, side], seq=right).wait_recv()
 
     def rim(m, side):
         src = conv_in.at[m, pl.ds(frames if side == 0 else 8, 8)]
@@ -229,7 +253,8 @@
         length = lengths[m]
         span = 3 * frames
         query = positions((frames, span), 0)
-        key = positions((frames, span), 1)
+        column = positions((frames, span), 1)
+        key = jnp.where(column < 2 * frames, column + near_keys, column + (far_keys - 2 * frames))
         place = seq * frames - frames + key
         allowed = (place >= 0) & (place < length) & (key >= query) & (key <= query + 2 * frames)
         mask[...] = jnp.where(allowed, 0.0, masked_score).astype(F32)
@@ -266,37 +291,50 @@
         for start in range(0, heads_width, 256):
             value = jnp.dot(normed[...], qkv_full[:, start : start + 256], preferred_element_type=F32)
             queries[:, start : start + 256] = value.astype(BF16)
-        for unit in range(len(units)):
-            for side in range(2):
-                halo(m, unit, side).wait_recv()
-
-        scale = 1.0 / head_size**0.5
-        for group in range(HEADS // 4):
-            base = group * 4 * head_size
-            outs = []
-            for h in range(4):
-                low, high = h * head_size, (h + 1) * head_size
-                lane_low, lane_high = low // 128 * 128, -(-high // 128) * 128
+        windows = []
+        for h in range(HEADS):
+            base, low = h // 4 * 4 * head_size, h % 4 * head_size
+            windows.append((base, low, low + head_size, low // 128 * 128, -(-(low + head_size) // 128) * 128))
+
+        def score(first_key, count, at):
+            for h, (base, low, high, lane_low, lane_high) in enumerate(windows):
                 lane = positions((frames, lane_high - lane_low), 1) + lane_low
                 q = queries[:, base + lane_low : base + lane_high]
                 q = jnp.where((lane >= low) & (lane < high), q, jnp.zeros_like(q))
-                k = kv[m, :, base + lane_low : base + lane_high]
-                v = kv[m, :, heads_width + base + lane_low : heads_width + base + lane_high]
-                scores = lax.dot_general(q, k, (((1,), (1,)), ((), ())), preferred_element_type=F32)
-                scores = scores * scale + mask[...]
-                highest = jnp.max(scores, axis=-1, keepdims=True)
-                expon = jnp.exp(scores - highest)
+                k = kv[m, pl.ds(first_key, count), base + lane_low : base + lane_high]
+                scores[h, :, at : at + count] = lax.dot_general(
+                    q, k, (((1,), (1,)), ((), ())), preferred_element_type=F32
+                )
+
+        halo_wait(m, near_side)
+        score(near_keys, 2 * frames, 0)
+        halo_wait(m, far_side)
+        score(far_keys, frames, 2 * frames)
+
+        scale = 1.0 / head_size**0.5
+        lane = positions((frames, 128), 1)
+        for group in range(HEADS // 4):
+            outs = []
+            for h in range(4 * group, 4 * group + 4):
+                base, low, high, lane_low, lane_high = windows[h]
+                columns = slice(heads_width + base + lane_low, heads_width + base + lane_high)
+                value = scores[h] * scale + mask[...]
+                expon = jnp.exp(value - jnp.max(value, axis=-1, keepdims=True))
                 total = jnp.sum(expon, axis=-1, keepdims=True)
-                probs = (expon * (1.0 / total)).astype(BF16)
-                outs.append(jnp.dot(probs, v, preferred_element_type=F32))
-            lane = positions((frames, 128), 1)
+                probs = expon.astype(BF16)
+                value = jnp.dot(
+                    probs[:, : 2 * frames], kv[m, pl.ds(near_keys, 2 * frames), columns], preferred_element_type=F32
+                ) + jnp.dot(
+                    probs[:, 2 * frames :], kv[m, pl.ds(far_keys, frames), columns], preferred_element_type=F32
+                )
+                outs.append(value * (1.0 / total))
             tiles = [
                 jnp.where(lane < 96, outs[0], outs[1][:, :128]),
                 jnp.where(lane < 64, outs[1][:, 128:], outs[2][:, :128]),
                 jnp.where(lane < 32, outs[2][:, 128:], outs[3]),
             ]
             for index, tile in enumerate(tiles):
-                at = base + index * 128
+                at = 4 * head_size * group + index * 128
                 context[:, at : at + 128] = tile.astype(BF16)
 
         @pl.when(m == 0)
@@ -377,6 +415,7 @@
             pltpu.VMEM((frames, heads_width), BF16),
             pltpu.VMEM((frames, heads_width), BF16),
             pltpu.VMEM((frames, 3 * frames), F32),
+            pltpu.VMEM((HEADS, frames, 3 * frames), F32),
             pltpu.VMEM((frames, width), F32),
             pltpu.VMEM((micro, frames + 16, width), F32),
             pltpu.VMEM((micro, frames, width), BF16),
@@ -387,6 +426,8 @@
             dma((4, 2, steps)),
             dma((4, 2 * steps)),
             dma((4, 2 * steps)),
+            dma((2 * steps,)),
+            dma((2 * steps,)),
             dma((micro, 4, 2)),
             dma((micro, 4, 2)),
             dma((micro, 2)),

time: 245 us -> 226 us (0.922)
  Pallas kernels: 242 us -> 222 us
    pallas_call x1, Pallas kernels: 242 us -> 222 us  [shards(): pl.pallas_call(functools.partial(kernel, sections, nseq), out_shape=jax.S...]
where the time goes in v3:
time: 226 us; the launch traced here: 225 us
  Pallas kernels  222 us (98%)
  local copies, waits for them, and re-layouts  2.85 us (1%)
    pallas_call x1, Pallas kernels, shards(): pl.pallas_call(functools.partial(kernel, sections, nseq), out_shape=jax.S...  222 us

profile of v3, /device:TPU:1, one launch (start us, length us, event | category | flops | bytes accessed | tf_op | source)
XLA Modules:
  0.0 224.8 jit_solution(5230340220954294886)
XLA Ops:
  0.0 0.8 copy.10
  0.8 0.0 copy-start
  0.8 0.0 copy-start.1
  0.8 0.0 copy-start.2
  0.8 0.0 copy-start.3
  0.8 0.0 copy-start.4
  0.8 1.2 reshape.3.grouped
  2.0 0.0 copy-done
  2.0 0.0 copy-done.1
  2.0 0.0 copy-done.2
  2.0 0.0 copy-done.3
  2.0 0.0 copy-done.4
  2.0 221.9 %shard_map.73 = bf16[2,128,1536]{2,1,0:T(8,128)(2,1)S(1)} custom-call(s32[2]{0:T(128)S(1)} %copy-done.4, bf16[2,128,512]{2,1,0:T(8,128)(2,1)S(1)} %reshape.3.grouped, bf16[16,1536]{1,0:T(8,128)(2,1)S(1)} %copy-done.2, bf16[48,2304]{1,0:T(8,128)(2,1)S(1)} %bitcast.8, bf16[24,1536]{1,0:T(8,128)(2,1)S(1)} %bitcast.10, f32[2,1536]{1,0:T(2,128)S(1)} %bitcast.11, ...), custom_call_target="tpu_custom_call" | custom-call | tf_op jit(solution)/shard_map/pallas_call | solution.py:402
  223.9 0.9 copy.12
Async XLA Ops:
  0.8 1.2 copy-start
  0.8 1.2 copy-start.1
  0.8 1.2 copy-start.2
  0.8 1.2 copy-start.3
  0.8 1.2 copy-start.4

commit v4 on v3

--- a/solution.py
+++ b/solution.py
@@ -9,6 +9,10 @@
 
 HEADS = 8
 STRIDE = 4
+UNITS = ((16, 16), (32, 16), (48, 32), (80, 32), (0, 16), (112, 16))
+DETOURS = 2
+RIM_UNIT = 4
+GROUPS = ((2,), (3, 0), (1, 4, 5))
 eps = 1e-05
 masked_score = -1e30
 F32 = jnp.float32
@@ -29,9 +33,9 @@
 def kernel(
     sections, nseq,
     lengths, grouped, stem_in, qkv_in, out_in, gains, taps, arrivals,
-    stem_full, qkv_full, out_full, out_peer, xs, normed, kv, queries, context, mask, scores, stream, conv_in, result,
+    stem_full, qkv_full, out_full, out_peer, xs, normed, kv, queries, context, mask, scores, stream, conv_in, result, passing,
     local_sem, pair_send, pair_recv, ring_send, ring_recv, cross_send, cross_recv, pass_send, pass_recv,
-    halo_send, halo_recv, rim_send, rim_recv, relay_send, relay_recv, done_sem,
+    halo_send, halo_recv, rim_send, rim_recv, relay_send, relay_recv, passing_send, passing_recv, done_sem,
 ):
     section = lax.axis_index("section")
     seq = lax.axis_index("seq")
@@ -44,6 +48,8 @@
     right, left = lax.rem(seq + 1, nseq), lax.rem(seq + nseq - 1, nseq)
     far = jnp.where(core == 1, right, left)
     following, preceding = lax.rem(section + 1, sections), lax.rem(section + sections - 1, sections)
+    partner = lax.rem(section + sections // 2, sections)
+    beside_following, beside_source = lax.rem(partner + 1, sections), lax.rem(partner + sections - 1, sections)
     first = section == 0
 
     micro, frames, width = xs.shape[0] // 2, xs.shape[1], xs.shape[2]
@@ -55,9 +61,10 @@
     for device in (
         {"seq": ahead}, {"seq": behind}, {"seq": other}, {"seq": far},
         {"dp": 1 - dp}, {"section": following}, {"section": preceding},
+        {"section": partner}, {"section": beside_following}, {"section": beside_source},
     ):
         pl.semaphore_signal(barrier, inc=1, device_id=device, device_id_type=MESH)
-    pl.semaphore_wait(barrier, 7)
+    pl.semaphore_wait(barrier, 10)
 
     def own_rows(full, count):
         return rows(full, (seq * 2 + dp) * count, count)
@@ -93,7 +100,7 @@
     hops, crosses, pairs = {}, {}, {}
     for name, (index, full, count, low, size, cut) in arrays.items():
         for side in range(2):
-            for t in range(1 if name == "peer" else steps):
+            for t in range(0 if name == "peer" else steps):
                 start, length = places[side][t] * (2 * count) + low, size
                 if t == steps - 1:
                     start, length = (start, cut) if side == 0 else (start + cut, size - cut)
@@ -107,7 +114,7 @@
             place = places[0][slot] if slot <= steps else places[1][slot - steps]
             src = rows(full, place * (2 * count) + low, size)
             crosses[name, slot] = remote(src, src, cross_send.at[index, slot], cross_recv.at[index, slot], seq=other)
-            if name == "own" and slot not in (0, 1, steps + 1):
+            if name == "own" and slot not in (0,):
                 pairs[slot] = remote(src, src, pass_send.at[slot], pass_recv.at[slot], dp=1 - dp)
 
     def hop(name, side, t):
@@ -118,7 +125,8 @@
 
     def ring_open(name):
         for side in range(2):
-            hop(name, side, 0).start()
+            if hop(name, side, 0) is not None:
+                hop(name, side, 0).start()
         cross(name, 0).start()
 
     def ring_step(name, t):
@@ -189,14 +197,27 @@
         [jnp.where(dp == 0, mine, theirs), jnp.where(dp == 0, theirs, mine)], axis=0
     )
     out_full[pl.ds(pl.multiple_of(seq * 2 * out_rows, 16), 2 * out_rows)] = both
+
+    @pl.when(first)
+    def _():
+        ring_step("stem", 1)
+
+    ring_step("own", 1)
     ring_open("out")
-    for t in range(1, steps):
-        @pl.when(first)
-        def _():
-            ring_step("stem", t)
-
-        for name in ("own", "peer", "out") if t == 1 else ("own", "out"):
-            ring_step(name, t)
+
+    @pl.when(first)
+    def _():
+        ring_step("stem", 2)
+
+    ring_step("own", 2)
+    ring_step("out", 1)
+
+    @pl.when(first)
+    def _():
+        ring_step("stem", 3)
+
+    ring_step("own", 3)
+    ring_step("out", 2)
 
     @pl.when(first)
     def _():
@@ -206,16 +227,37 @@
 
     ring_close("own")
     ring_close("peer")
-
-    units = ((16, frames // 2 - 16), (frames // 2, frames // 2 - 16), (0, 16), (frames - 16, 16))
-    groups = ((0,), (1,), (2, 3))
+    ring_step("out", 3)
+
+    units = UNITS
+    groups = GROUPS
 
     def relay(m, unit):
         start, count = units[unit]
-        return remote(
-            result.at[m, pl.ds(start, count)], xs.at[m, pl.ds(start, count)],
-            relay_send.at[m, unit], relay_recv.at[m, unit], section=following,
-        )
+        src = result.at[m, pl.ds(start, count)]
+        if unit < DETOURS:
+            dst = passing.at[m, pl.ds(start - units[0][0], count)]
+            return remote(src, dst, relay_send.at[m, unit], passing_recv.at[m, unit], section=beside_following)
+        dst = xs.at[m, pl.ds(start, count)]
+        return remote(src, dst, relay_send.at[m, unit], relay_recv.at[m, unit], section=following)
+
+    def onward(m, unit):
+        start, count = units[unit]
+        src = passing.at[m, pl.ds(start - units[0][0], count)]
+        dst = xs.at[m, pl.ds(start, count)]
+        return remote(src, dst, passing_send.at[m, unit], relay_recv.at[m, unit], section=partner)
+
+    def arrive(m, unit):
+        (onward if unit < DETOURS else relay)(m, unit).wait_recv()
+
+    def pass_on():
+        def one(m, carry):
+            for unit in range(DETOURS):
+                relay(m, unit).wait_recv()
+                onward(m, unit).start()
+            return carry
+
+        lax.fori_loop(0, micro, one, 0)
 
     def halo(m, unit, side):
         start, count = units[unit]
@@ -264,7 +306,7 @@
             @pl.when(jnp.logical_not(first))
             def _():
                 for unit in group:
-                    relay(m, unit).wait_recv()
+                    arrive(m, unit)
 
             for unit in group:
                 for start in range(units[unit][0], sum(units[unit]), 16):
@@ -352,7 +394,7 @@
             rim(m, side).start()
         count = taps.shape[0]
         for unit in range(len(units)):
-            if unit == 2:
+            if unit == RIM_UNIT:
                 for side in range(2):
                     rim(m, side).wait_recv()
                 top, bottom = conv_in[m, 0:8, :], conv_in[m, 8 + frames : 16 + frames, :]
@@ -368,13 +410,21 @@
             relay(m, unit).start()
         return carry
 
+    @pl.when(section > sections // 2)
+    def _():
+        pass_on()
+
     lax.fori_loop(0, micro, layer, 0)
+
+    @pl.when(section <= sections // 2)
+    def _():
+        pass_on()
 
     @pl.when(first)
     def _():
         for m in range(micro):
             for unit in range(len(units)):
-                relay(m, unit).wait_recv()
+                arrive(m, unit)
             keep(m).start()
 
     for name in ("own", "peer", "out"):
@@ -382,6 +432,8 @@
     for m in range(micro):
         for unit in range(len(units)):
             relay(m, unit).wait_send()
+            if unit < DETOURS:
+                onward(m, unit).wait_send()
             for side in range(2):
                 halo(m, unit, side).wait_send()
         for side in range(2):
@@ -419,6 +471,7 @@
             pltpu.VMEM((frames, width), F32),
             pltpu.VMEM((micro, frames + 16, width), F32),
             pltpu.VMEM((micro, frames, width), BF16),
+            pltpu.VMEM((micro, sum(count for _, count in UNITS[:DETOURS]), width), BF16),
             dma((2,)),
             dma((3,)),
             dma((3,)),
@@ -428,12 +481,14 @@
             dma((4, 2 * steps)),
             dma((2 * steps,)),
             dma((2 * steps,)),
-            dma((micro, 4, 2)),
-            dma((micro, 4, 2)),
+            dma((micro, len(UNITS), 2)),
+            dma((micro, len(UNITS), 2)),
             dma((micro, 2)),
             dma((micro, 2)),
-            dma((micro, 4)),
-            dma((micro, 4)),
+            dma((micro, len(UNITS))),
+            dma((micro, len(UNITS))),
+            dma((micro, DETOURS)),
+            dma((micro, DETOURS)),
             dma((micro,)),
         ],
         compiler_params=pltpu.CompilerParams(

time: 226 us -> 209 us (0.925)
  Pallas kernels: 222 us -> 206 us
    pallas_call x1, Pallas kernels: 222 us -> 206 us  [shards(): pl.pallas_call(functools.partial(kernel, sections, nseq), out_shape=jax.S...]
where the time goes in v4:
time: 209 us
  Pallas kernels  206 us (99%)
  local copies, waits for them, and re-layouts  2.85 us (1%)
    pallas_call x1, Pallas kernels, shards(): pl.pallas_call(functools.partial(kernel, sections, nseq), out_shape=jax.S...  206 us

profile of v4, /device:TPU:1, one launch (start us, length us, event | category | flops | bytes accessed | tf_op | source)
XLA Modules:
  0.0 208.5 jit_solution(14339751373383498692)
XLA Ops:
  0.0 0.8 copy.10
  0.8 0.0 copy-start
  0.8 0.0 copy-start.1
  0.8 0.0 copy-start.2
  0.8 0.0 copy-start.3
  0.8 0.0 copy-start.4
  0.8 1.2 reshape.3.grouped
  2.0 0.0 copy-done
  2.0 0.0 copy-done.1
  2.0 0.0 copy-done.2
  2.0 0.0 copy-done.3
  2.0 0.0 copy-done.4
  2.0 205.6 %shard_map.73 = bf16[2,128,1536]{2,1,0:T(8,128)(2,1)S(1)} custom-call(s32[2]{0:T(128)S(1)} %copy-done.4, bf16[2,128,512]{2,1,0:T(8,128)(2,1)S(1)} %reshape.3.grouped, bf16[16,1536]{1,0:T(8,128)(2,1)S(1)} %copy-done.2, bf16[48,2304]{1,0:T(8,128)(2,1)S(1)} %bitcast.8, bf16[24,1536]{1,0:T(8,128)(2,1)S(1)} %bitcast.10, f32[2,1536]{1,0:T(2,128)S(1)} %bitcast.11, ...), custom_call_target="tpu_custom_call" | custom-call | tf_op jit(solution)/shard_map/pallas_call | solution.py:454
  207.7 0.9 copy.12
Async XLA Ops:
  0.8 1.2 copy-start
  0.8 1.2 copy-start.1
  0.8 1.2 copy-start.2
  0.8 1.2 copy-start.3
  0.8 1.2 copy-start.4

commit v5 on v4

--- a/solution.py
+++ b/solution.py
@@ -13,6 +13,12 @@
 DETOURS = 2
 RIM_UNIT = 4
 GROUPS = ((2,), (3, 0), (1, 4, 5))
+PIECES = tuple(
+    (unit, part, parts)
+    for group in GROUPS
+    for part, parts in (((0, 1), (1, 1)) if group == GROUPS[-1] else ((0, 2),))
+    for unit in group
+)
 eps = 1e-05
 masked_score = -1e30
 F32 = jnp.float32
@@ -32,9 +38,9 @@
 
 def kernel(
     sections, nseq,
-    lengths, grouped, stem_in, qkv_in, out_in, gains, taps, arrivals,
+    lengths, mel, stem_in, qkv_in, out_in, gains, taps, arrivals,
     stem_full, qkv_full, out_full, out_peer, xs, normed, kv, queries, context, mask, scores, stream, conv_in, result, passing,
-    local_sem, pair_send, pair_recv, ring_send, ring_recv, cross_send, cross_recv, pass_send, pass_recv,
+    mel_wide, local_sem, stem_send, stem_recv, pair_send, pair_recv, ring_send, ring_recv, cross_send, cross_recv, pass_send, pass_recv,
     halo_send, halo_recv, rim_send, rim_recv, relay_send, relay_recv, passing_send, passing_recv, done_sem,
 ):
     section = lax.axis_index("section")
@@ -51,6 +57,7 @@
     partner = lax.rem(section + sections // 2, sections)
     beside_following, beside_source = lax.rem(partner + 1, sections), lax.rem(partner + sections - 1, sections)
     first = section == 0
+    makes_stem = section == sections // 2 - 1
 
     micro, frames, width = xs.shape[0] // 2, xs.shape[1], xs.shape[2]
     heads_width = queries.shape[1]
@@ -75,7 +82,7 @@
     qkv_keep = pltpu.make_async_copy(qkv_in, own_rows(qkv_full, qkv_rows), local_sem.at[0])
     out_pair = remote(out_in, out_peer, pair_send.at[1], pair_recv.at[1], dp=1 - dp)
 
-    @pl.when(first)
+    @pl.when(makes_stem)
     def _():
         stem_pair.start()
         stem_keep.start()
@@ -100,9 +107,9 @@
     hops, crosses, pairs = {}, {}, {}
     for name, (index, full, count, low, size, cut) in arrays.items():
         for side in range(2):
-            for t in range(0 if name == "peer" else steps):
+            for t in ((steps - 2,) if name == "peer" else range(steps)):
                 start, length = places[side][t] * (2 * count) + low, size
-                if t == steps - 1:
+                if t == steps - 1 and name != "peer":
                     start, length = (start, cut) if side == 0 else (start + cut, size - cut)
                 if length:
                     src = rows(full, start, length)
@@ -114,7 +121,7 @@
             place = places[0][slot] if slot <= steps else places[1][slot - steps]
             src = rows(full, place * (2 * count) + low, size)
             crosses[name, slot] = remote(src, src, cross_send.at[index, slot], cross_recv.at[index, slot], seq=other)
-            if name == "own" and slot not in (0,):
+            if name == "own" and slot not in (0, steps - 1, 2 * steps - 1):
                 pairs[slot] = remote(src, src, pass_send.at[slot], pass_recv.at[slot], dp=1 - dp)
 
     def hop(name, side, t):
@@ -149,10 +156,15 @@
             pairs[steps].start()
         if name != "peer":
             cross(name, steps).start()
-        for slot in range(2 * steps):
-            if name == "peer" and slot in pairs:
+        if name == "peer":
+            for slot in [t + side * steps for t in range(1, steps - 1) for side in range(2)] + [steps]:
                 pairs[slot].wait_recv()
                 cross(name, slot).start()
+                if slot in (steps - 2, 2 * steps - 2):
+                    hop(name, slot // steps, steps - 2).start()
+            for side in range(2):
+                hop(name, side, steps - 2).wait_recv()
+                cross(name, steps - 1 + side * steps).start()
         for slot in range(2 * steps):
             cross(name, slot).wait_recv()
 
@@ -173,21 +185,32 @@
     def valid_rows(m, start, count):
         return jnp.where(positions((count, 1), 0) < lengths[m] - seq * frames - start, 1.0, 0.0)
 
-    def stem():
-        for m in range(micro):
-            for start in range(0, width, 256):
-                value = jnp.dot(grouped[m], stem_full[:, start : start + 256], preferred_element_type=F32)
-                value = value * jax.nn.sigmoid(value) * valid_rows(m, 0, frames)
-                xs[micro + m, :, start : start + 256] = value.astype(BF16)
-
-    qkv_keep.wait()
-    ring_open("own")
-
-    @pl.when(first)
+    def stem_copy(m):
+        whole = xs.at[micro + m]
+        return remote(whole, whole, stem_send.at[m], stem_recv.at[m], section=beside_following)
+
+    @pl.when(makes_stem)
     def _():
         stem_keep.wait()
         stem_pair.wait()
         ring_open("stem")
+        for t in range(1, steps):
+            ring_step("stem", t)
+        ring_close("stem")
+        for m in range(micro):
+            mel_wide[...] = mel[m].astype(F32)
+            joined = jnp.concatenate(
+                [mel_wide[pl.ds(step, frames, stride=STRIDE), :].astype(BF16) for step in range(STRIDE)], axis=1
+            )
+            for start in range(0, width, 256):
+                value = jnp.dot(joined, stem_full[:, start : start + 256], preferred_element_type=F32)
+                value = value * jax.nn.sigmoid(value) * valid_rows(m, 0, frames)
+                xs[micro + m, :, start : start + 256] = value.astype(BF16)
+            stem_copy(m).start()
+        ring_sent("stem")
+
+    qkv_keep.wait()
+    ring_open("own")
 
     qkv_pair.wait()
     ring_open("peer")
@@ -198,36 +221,23 @@
     )
     out_full[pl.ds(pl.multiple_of(seq * 2 * out_rows, 16), 2 * out_rows)] = both
 
-    @pl.when(first)
-    def _():
-        ring_step("stem", 1)
-
     ring_step("own", 1)
     ring_open("out")
 
-    @pl.when(first)
-    def _():
-        ring_step("stem", 2)
-
     ring_step("own", 2)
     ring_step("out", 1)
 
-    @pl.when(first)
-    def _():
-        ring_step("stem", 3)
-
     ring_step("own", 3)
     ring_step("out", 2)
-
-    @pl.when(first)
-    def _():
-        ring_close("stem")
-        stem()
-        ring_sent("stem")
 
     ring_close("own")
     ring_close("peer")
     ring_step("out", 3)
+
+    @pl.when(jnp.logical_not(first))
+    def _():
+        ring_close("out")
+
 
     units = UNITS
     groups = GROUPS
@@ -259,23 +269,28 @@
 
         lax.fori_loop(0, micro, one, 0)
 
-    def halo(m, unit, side):
+    def halo(m, index, side):
+        unit, part, parts = PIECES[index]
         start, count = units[unit]
-        src = kv.at[m, pl.ds(frames + start, count)]
-        dst = kv.at[m, pl.ds(2 * frames * side + start, count)]
+        columns = pl.ds(part * heads_width, parts * heads_width)
+        src = kv.at[m, pl.ds(frames + start, count), columns]
+        dst = kv.at[m, pl.ds(2 * frames * side + start, count), columns]
         return remote(
-            src, dst, halo_send.at[m, unit, side], halo_recv.at[m, unit, side], seq=right if side == 0 else left
+            src, dst, halo_send.at[m, index, side], halo_recv.at[m, index, side], seq=right if side == 0 else left
         )
 
     near_side, far_side = 1 - core, core
     near_keys = pl.multiple_of(frames * (1 - core), 128)
     far_keys = pl.multiple_of(2 * frames * core, 128)
 
-    def halo_wait(m, side):
-        for unit, (start, count) in enumerate(units):
-            src = kv.at[m, pl.ds(frames + start, count)]
-            dst = rows(kv.at[m], 2 * frames * side + start, count)
-            remote(src, dst, halo_send.at[m, unit, side], halo_recv.at[m, unit, side], seq=right).wait_recv()
+    def halo_wait(m, side, wanted):
+        for index, (unit, part, parts) in enumerate(PIECES):
+            if part == wanted:
+                start, count = units[unit]
+                columns = pl.ds(part * heads_width, parts * heads_width)
+                src = kv.at[m, pl.ds(frames + start, count), columns]
+                dst = kv.at[m, pl.ds(pl.multiple_of(2 * frames * side + start, 16), count), columns]
+                remote(src, dst, halo_send.at[m, index, side], halo_recv.at[m, index, side], seq=right).wait_recv()
 
     def rim(m, side):
         src = conv_in.at[m, pl.ds(frames if side == 0 else 8, 8)]
@@ -302,6 +317,11 @@
         mask[...] = jnp.where(allowed, 0.0, masked_score).astype(F32)
 
         slot = jnp.where(first, micro + m, m)
+
+        @pl.when(first)
+        def _():
+            stem_copy(m).wait_recv()
+
         for group in groups:
             @pl.when(jnp.logical_not(first))
             def _():
@@ -314,17 +334,19 @@
                     normed[start : start + 16, :] = norm(value, gains[0:1, :]).astype(BF16)
             some = [normed[units[unit][0] : sum(units[unit]), :] for unit in group]
             some = some[0] if len(some) == 1 else jnp.concatenate(some, axis=0)
-            for start in range(0, 2 * heads_width, 256):
-                at = heads_width + start
-                value = jnp.dot(some, qkv_full[:, at : at + 256], preferred_element_type=F32).astype(BF16)
-                low = 0
-                for unit in group:
-                    at, count = units[unit]
-                    kv[m, frames + at : frames + at + count, start : start + 256] = value[low : low + count]
-                    low += count
-            for unit in group:
-                for side in range(2):
-                    halo(m, unit, side).start()
+            for part in range(2):
+                for start in range(part * heads_width, (part + 1) * heads_width, 256):
+                    at = heads_width + start
+                    value = jnp.dot(some, qkv_full[:, at : at + 256], preferred_element_type=F32).astype(BF16)
+                    low = 0
+                    for unit in group:
+                        at, count = units[unit]
+                        kv[m, frames + at : frames + at + count, start : start + 256] = value[low : low + count]
+                        low += count
+                for index, (unit, first_part, parts) in enumerate(PIECES):
+                    if unit in group and first_part + parts - 1 == part:
+                        for side in range(2):
+                            halo(m, index, side).start()
 
         @pl.when(jnp.logical_not(first))
         def _():
@@ -348,10 +370,12 @@
                     q, k, (((1,), (1,)), ((), ())), preferred_element_type=F32
                 )
 
-        halo_wait(m, near_side)
+        halo_wait(m, near_side, 0)
         score(near_keys, 2 * frames, 0)
-        halo_wait(m, far_side)
+        halo_wait(m, far_side, 0)
         score(far_keys, frames, 2 * frames)
+        halo_wait(m, near_side, 1)
+        halo_wait(m, far_side, 1)
 
         scale = 1.0 / head_size**0.5
         lane = positions((frames, 128), 1)
@@ -379,7 +403,7 @@
                 at = 4 * head_size * group + index * 128
                 context[:, at : at + 128] = tile.astype(BF16)
 
-        @pl.when(m == 0)
+        @pl.when(first & (m == 0))
         def _():
             ring_close("out")
 
@@ -387,11 +411,20 @@
             value = jnp.dot(context[...], out_full[:, start : start + 256], preferred_element_type=F32)
             stream[:, start : start + 256] = value + xs[slot, :, start : start + 256].astype(F32)
 
-        for start in range(0, frames, 16):
-            value = norm(stream[start : start + 16, :], gains[1:2, :]) * valid_rows(m, start, 16)
-            conv_in[m, 8 + start : 8 + start + 16, :] = value.astype(BF16).astype(F32)
+        ready = set()
+
+        def prepare(starts):
+            for start in starts:
+                if start in ready or not 0 <= start < frames:
+                    continue
+                ready.add(start)
+                value = norm(stream[start : start + 16, :], gains[1:2, :]) * valid_rows(m, start, 16)
+                conv_in[m, 8 + start : 8 + start + 16, :] = value.astype(BF16).astype(F32)
+
+        prepare((0, frames - 16))
         for side in range(2):
             rim(m, side).start()
+
         count = taps.shape[0]
         for unit in range(len(units)):
             if unit == RIM_UNIT:
@@ -401,6 +434,7 @@
                 conv_in[m, 0:8, :] = jnp.where(seq == 0, 0.0, top)
                 conv_in[m, 8 + frames : 16 + frames, :] = jnp.where(seq == nseq - 1, 0.0, bottom)
             for start in range(units[unit][0], sum(units[unit]), 16):
+                prepare((start - 16, start, start + 16))
                 conv = jnp.zeros((16, width), F32)
                 for offset in range(count):
                     at = 8 - count // 2 + start + offset
@@ -427,6 +461,11 @@
                 arrive(m, unit)
             keep(m).start()
 
+    @pl.when(makes_stem)
+    def _():
+        for m in range(micro):
+            stem_copy(m).wait_send()
+
     for name in ("own", "peer", "out"):
         ring_sent(name)
     for m in range(micro):
@@ -434,10 +473,10 @@
             relay(m, unit).wait_send()
             if unit < DETOURS:
                 onward(m, unit).wait_send()
-            for side in range(2):
-                halo(m, unit, side).wait_send()
         for side in range(2):
             rim(m, side).wait_send()
+            for index in range(len(PIECES)):
+                halo(m, index, side).wait_send()
         keep(m).wait()
 
 
@@ -446,7 +485,6 @@
     frames = mel.shape[1] // STRIDE
     width = stem_weight.shape[1]
     heads_width = w_qkv.shape[2] // 3
-    grouped = mel.reshape(micro, frames, STRIDE * mel.shape[2])
     depth, full_out = w_qkv.shape[1] * 2 * nseq, w_out.shape[1] * 2 * nseq
     steps = nseq // 4
     dma = pltpu.SemaphoreType.DMA
@@ -472,7 +510,10 @@
             pltpu.VMEM((micro, frames + 16, width), F32),
             pltpu.VMEM((micro, frames, width), BF16),
             pltpu.VMEM((micro, sum(count for _, count in UNITS[:DETOURS]), width), BF16),
+            pltpu.VMEM(mel.shape[1:], F32),
             dma((2,)),
+            dma((micro,)),
+            dma((micro,)),
             dma((3,)),
             dma((3,)),
             dma((4, 2, steps)),
@@ -481,8 +522,8 @@
             dma((4, 2 * steps)),
             dma((2 * steps,)),
             dma((2 * steps,)),
-            dma((micro, len(UNITS), 2)),
-            dma((micro, len(UNITS), 2)),
+            dma((micro, len(PIECES), 2)),
+            dma((micro, len(PIECES), 2)),
             dma((micro, 2)),
             dma((micro, 2)),
             dma((micro, len(UNITS))),
@@ -494,7 +535,7 @@
         compiler_params=pltpu.CompilerParams(
             collective_id=0, has_side_effects=True, vmem_limit_bytes=48 * 1024 * 1024
         ),
-    )(lengths, grouped, stem_weight, w_qkv[0], w_out[0], norm_gains[0], conv_kernel[0])
+    )(lengths, mel, stem_weight, w_qkv[0], w_out[0], norm_gains[0], conv_kernel[0])
     return arrived[None]
 
 

time: 209 us -> 195 us (0.933)
  Pallas kernels: 206 us -> 190 us
  local copies, waits for them, and re-layouts: 2.85 us -> 5.02 us
    pallas_call x1, Pallas kernels: 206 us -> 190 us  [shards(): pl.pallas_call(functools.partial(kernel, sections, nseq), out_shape=jax.S...]
    unnamed x12 -> x14, local copies, waits for them, and re-layouts: 1.67 us -> 5.02 us
where the time goes in v5:
time: 195 us
  Pallas kernels  190 us (97%)
  local copies, waits for them, and re-layouts  5.02 us (3%)
    pallas_call x1, Pallas kernels, shards(): pl.pallas_call(functools.partial(kernel, sections, nseq), out_shape=jax.S...  190 us
    unnamed x14, local copies, waits for them, and re-layouts  5.02 us

profile of v5, /device:TPU:1, one launch (start us, length us, event | category | flops | bytes accessed | tf_op | source)
XLA Modules:
  0.0 195.1 jit_solution(16251071489407455768)
XLA Ops:
  0.0 0.0 copy-start.2
  0.0 0.0 copy-start.4
  0.0 0.8 copy.10
  0.8 0.0 copy-start.5
  0.8 0.1 copy-done.2
  0.9 0.0 copy-done.4
  0.9 0.6 copy-done.5
  1.5 0.0 copy-start
  1.5 0.9 copy-done
  2.4 0.0 copy-start.1
  2.4 0.9 copy-done.1
  3.3 0.0 copy-start.3
  3.3 0.8 copy-done.3
  4.1 190.1 %shard_map.73 = bf16[2,128,1536]{2,1,0:T(8,128)(2,1)S(1)} custom-call(s32[2]{0:T(128)S(1)} %copy-done.5, bf16[2,512,128]{2,1,0:T(8,128)(2,1)S(1)} %copy-done, bf16[16,1536]{1,0:T(8,128)(2,1)S(1)} %copy-done.3, bf16[48,2304]{1,0:T(8,128)(2,1)S(1)} %bitcast.8, bf16[24,1536]{1,0:T(8,128)(2,1)S(1)} %bitcast.10, f32[2,1536]{1,0:T(2,128)S(1)} %bitcast.11, ...), custom_call_target="tpu_custom_call" | custom-call | tf_op jit(solution)/shard_map/pallas_call | solution.py:492
  194.2 0.9 copy.12
Async XLA Ops:
  0.0 0.9 copy-start.2
  0.0 0.9 copy-start.4
  0.8 0.7 copy-start.5
  1.5 0.9 copy-start
  2.4 0.9 copy-start.1
  3.3 0.8 copy-start.3

commit v6 on v5

--- a/solution.py
+++ b/solution.py
@@ -100,7 +100,7 @@
     out_cut = out_rows // 16 * 16
     arrays = {
         "stem": (0, stem_full, stem_rows, 0, 2 * stem_rows, stem_rows),
-        "own": (1, qkv_full, qkv_rows, dp * qkv_rows, qkv_rows, qkv_rows),
+        "own": (1, qkv_full, qkv_rows, dp * qkv_rows, qkv_rows, -(-qkv_rows // 32) * 16),
         "peer": (2, qkv_full, qkv_rows, (1 - dp) * qkv_rows, qkv_rows, qkv_rows),
         "out": (3, out_full, out_rows, 0, 2 * out_rows, out_cut),
     }
@@ -222,15 +222,12 @@
     out_full[pl.ds(pl.multiple_of(seq * 2 * out_rows, 16), 2 * out_rows)] = both
 
     ring_step("own", 1)
+    ring_step("own", 2)
     ring_open("out")
-
-    ring_step("own", 2)
+    ring_step("own", 3)
     ring_step("out", 1)
-
-    ring_step("own", 3)
+    ring_close("own")
     ring_step("out", 2)
-
-    ring_close("own")
     ring_close("peer")
     ring_step("out", 3)
 
@@ -366,12 +363,13 @@
                 q = queries[:, base + lane_low : base + lane_high]
                 q = jnp.where((lane >= low) & (lane < high), q, jnp.zeros_like(q))
                 k = kv[m, pl.ds(first_key, count), base + lane_low : base + lane_high]
-                scores[h, :, at : at + count] = lax.dot_general(
+                scores[h, :, pl.ds(at, count)] = lax.dot_general(
                     q, k, (((1,), (1,)), ((), ())), preferred_element_type=F32
                 )
 
+        score(frames, frames, pl.multiple_of(frames * core, 128))
         halo_wait(m, near_side, 0)
-        score(near_keys, 2 * frames, 0)
+        score(pl.multiple_of(2 * frames * (1 - core), 128), frames, pl.multiple_of(frames * (1 - core), 128))
         halo_wait(m, far_side, 0)
         score(far_keys, frames, 2 * frames)
         halo_wait(m, near_side, 1)

time: 195 us -> 194 us (level)
  no operation moved by 1% of the time
where the time goes in v6:
time: 194 us
  Pallas kernels  189 us (97%)
  local copies, waits for them, and re-layouts  5.02 us (3%)
    pallas_call x1, Pallas kernels, shards(): pl.pallas_call(functools.partial(kernel, sections, nseq), out_shape=jax.S...  189 us
    unnamed x14, local copies, waits for them, and re-layouts  5.02 us

profile of v6, /device:TPU:1, one launch (start us, length us, event | category | flops | bytes accessed | tf_op | source)
XLA Modules:
  0.0 193.8 jit_solution(11085541753740244632)
XLA Ops:
  0.0 0.0 copy-start.2
  0.0 0.0 copy-start.4
  0.0 0.8 copy.10
  0.8 0.0 copy-start.5
  0.8 0.1 copy-done.2
  0.9 0.0 copy-done.4
  0.9 0.6 copy-done.5
  1.5 0.0 copy-start
  1.5 0.9 copy-done
  2.4 0.0 copy-start.1
  2.4 0.9 copy-done.1
  3.3 0.0 copy-start.3
  3.3 0.8 copy-done.3
  4.1 188.8 %shard_map.73 = bf16[2,128,1536]{2,1,0:T(8,128)(2,1)S(1)} custom-call(s32[2]{0:T(128)S(1)} %copy-done.5, bf16[2,512,128]{2,1,0:T(8,128)(2,1)S(1)} %copy-done, bf16[16,1536]{1,0:T(8,128)(2,1)S(1)} %copy-done.3, bf16[48,2304]{1,0:T(8,128)(2,1)S(1)} %bitcast.8, bf16[24,1536]{1,0:T(8,128)(2,1)S(1)} %bitcast.10, f32[2,1536]{1,0:T(2,128)S(1)} %bitcast.11, ...), custom_call_target="tpu_custom_call" | custom-call | tf_op jit(solution)/shard_map/pallas_call | solution.py:490
  193.0 0.9 copy.12
Async XLA Ops:
  0.0 0.9 copy-start.2
  0.0 0.9 copy-start.4
  0.8 0.7 copy-start.5
  1.5 0.9 copy-start
  2.4 0.9 copy-start.1
  3.3 0.8 copy-start.3

commit v7 on v6

--- a/solution.py
+++ b/solution.py
@@ -39,7 +39,7 @@
 def kernel(
     sections, nseq,
     lengths, mel, stem_in, qkv_in, out_in, gains, taps, arrivals,
-    stem_full, qkv_full, out_full, out_peer, xs, normed, kv, queries, context, mask, scores, stream, conv_in, result, passing,
+    stem_full, qkv_full, out_full, out_peer, xs, normed, kv, queries, context, mask, scores, probs_all, stream, conv_in, result, passing,
     mel_wide, local_sem, stem_send, stem_recv, pair_send, pair_recv, ring_send, ring_recv, cross_send, cross_recv, pass_send, pass_recv,
     halo_send, halo_recv, rim_send, rim_recv, relay_send, relay_recv, passing_send, passing_recv, done_sem,
 ):
@@ -372,20 +372,23 @@
         score(pl.multiple_of(2 * frames * (1 - core), 128), frames, pl.multiple_of(frames * (1 - core), 128))
         halo_wait(m, far_side, 0)
         score(far_keys, frames, 2 * frames)
+
+        scale = 1.0 / head_size**0.5
+        totals = []
+        for h in range(HEADS):
+            value = scores[h] * scale + mask[...]
+            expon = jnp.exp(value - jnp.max(value, axis=-1, keepdims=True))
+            totals.append(jnp.sum(expon, axis=-1, keepdims=True))
+            probs_all[h] = expon.astype(BF16)
         halo_wait(m, near_side, 1)
         halo_wait(m, far_side, 1)
-
-        scale = 1.0 / head_size**0.5
         lane = positions((frames, 128), 1)
         for group in range(HEADS // 4):
             outs = []
             for h in range(4 * group, 4 * group + 4):
                 base, low, high, lane_low, lane_high = windows[h]
                 columns = slice(heads_width + base + lane_low, heads_width + base + lane_high)
-                value = scores[h] * scale + mask[...]
-                expon = jnp.exp(value - jnp.max(value, axis=-1, keepdims=True))
-                total = jnp.sum(expon, axis=-1, keepdims=True)
-                probs = expon.astype(BF16)
+                total, probs = totals[h], probs_all[h]
                 value = jnp.dot(
                     probs[:, : 2 * frames], kv[m, pl.ds(near_keys, 2 * frames), columns], preferred_element_type=F32
                 ) + jnp.dot(
@@ -504,6 +507,7 @@
             pltpu.VMEM((frames, heads_width), BF16),
             pltpu.VMEM((frames, 3 * frames), F32),
             pltpu.VMEM((HEADS, frames, 3 * frames), F32),
+            pltpu.VMEM((HEADS, frames, 3 * frames), BF16),
             pltpu.VMEM((frames, width), F32),
             pltpu.VMEM((micro, frames + 16, width), F32),
             pltpu.VMEM((micro, frames, width), BF16),

time: 194 us -> 192 us (0.990)
  Pallas kernels: 189 us -> 187 us
    pallas_call x1, Pallas kernels: 189 us -> 187 us  [shards(): pl.pallas_call(functools.partial(kernel, sections, nseq), out_shape=jax.S...]
where the time goes in v7:
time: 192 us
  Pallas kernels  187 us (97%)
  local copies, waits for them, and re-layouts  5.02 us (3%)
    pallas_call x1, Pallas kernels, shards(): pl.pallas_call(functools.partial(kernel, sections, nseq), out_shape=jax.S...  187 us
    unnamed x14, local copies, waits for them, and re-layouts  5.02 us

profile of v7, /device:TPU:1, one launch (start us, length us, event | category | flops | bytes accessed | tf_op | source)
XLA Modules:
  0.0 191.7 jit_solution(6619799943156504578)
XLA Ops:
  0.0 0.0 copy-start.2
  0.0 0.0 copy-start.4
  0.0 0.8 copy.10
  0.8 0.0 copy-start.5
  0.8 0.1 copy-done.2
  0.9 0.0 copy-done.4
  0.9 0.6 copy-done.5
  1.5 0.0 copy-start
  1.5 0.9 copy-done
  2.4 0.0 copy-start.1
  2.4 0.9 copy-done.1
  3.3 0.0 copy-start.3
  3.3 0.8 copy-done.3
  4.1 186.7 %shard_map.73 = bf16[2,128,1536]{2,1,0:T(8,128)(2,1)S(1)} custom-call(s32[2]{0:T(128)S(1)} %copy-done.5, bf16[2,512,128]{2,1,0:T(8,128)(2,1)S(1)} %copy-done, bf16[16,1536]{1,0:T(8,128)(2,1)S(1)} %copy-done.3, bf16[48,2304]{1,0:T(8,128)(2,1)S(1)} %bitcast.8, bf16[24,1536]{1,0:T(8,128)(2,1)S(1)} %bitcast.10, f32[2,1536]{1,0:T(2,128)S(1)} %bitcast.11, ...), custom_call_target="tpu_custom_call" | custom-call | tf_op jit(solution)/shard_map/pallas_call | solution.py:493
  190.9 0.9 copy.12
Async XLA Ops:
  0.0 0.9 copy-start.2
  0.0 0.9 copy-start.4
  0.8 0.7 copy-start.5
  1.5 0.9 copy-start
  2.4 0.9 copy-start.1
  3.3 0.8 copy-start.3
